TPU v7x, 32 devices: a whole 2x2x4 slice. The times are simulated.
32 devices in a mesh: segment: 2 (over x), dp: 4 (over z), mp: 4 (over y, core).
Axes of the slice: x: 2, y: 2, z: 4, core: 2. Of those that a mesh axis runs over, the one named last changes fastest.
Arguments:
- images: bfloat16 [8, 128, 3840], P(('segment', 'dp')), may hold values from -6 to 6
- ln_gain: float32 [1280], replicated, may hold values from 0.1 to 1.9
- projector: bfloat16 [3840, 8192], P(None, 'mp'), may hold values from -0.09375 to 0.09375
- tile_counts: int32 [8], P(('segment', 'dp')), may hold values from 1 to 4
- assign: int32 [8], P(('segment', 'dp')), may hold values from 0 to 7, as said below
- text: bfloat16 [8, 64, 8192], P('dp', None, 'mp'), may hold values from -6 to 6
- text_start: int32 [8], P('dp'), may hold values from 0 to 32
- w_query: bfloat16 [2, 8192, 4096], P('segment', 'mp'), may hold values from -0.0625 to 0.0625
- w_key: bfloat16 [2, 8192, 512], P('segment', 'mp'), may hold values from -0.0625 to 0.0625
- w_value: bfloat16 [2, 8192, 512], P('segment', 'mp'), may hold values from -0.0625 to 0.0625
- w_out: bfloat16 [2, 4096, 8192], P('segment', None, 'mp'), may hold values from -0.09375 to 0.09375
- gates: float32 [2], P('segment'), may hold values from -1.5 to 1.5
- grad_out: bfloat16 [8, 64, 8192], P('dp', None, 'mp'), may hold values from -6 to 6
Outputs:
- phase_grads: bfloat16 [2, 8, 64, 8192], P('segment', 'dp', None, 'mp')
- feature_grads: bfloat16 [8, 128, 3840], P(('segment', 'dp'))
Inputs may be any that keep to these rules, and one draw needn't show every extreme that they name: assign is a permutation of the 8 sequences; sequence j belongs to index j // 2 of dp, image e is encoded on index e // 4 of segment and index e % 4 of dp, and the images of one index of segment belong to sequences of 4 different indices of dp.
All inputs are finite; a program needn't handle non-finite values.
Results may differ from a plain program's by a relative error of at most 0.035.
Values may be sent and summed in bfloat16 or wider, within the bound.
A program may use at most 192 MiB of HBM per device.

v0:
```python
import functools

import jax
import jax.numpy as jnp
from jax import lax
from jax.experimental import pallas as pl
from jax.experimental.pallas import tpu as pltpu
from jax.sharding import PartitionSpec as P

HD = 128
PATCH = 32
CHUNKS = 2
LANES = 128
BACK_LANES = 512
BLOCK = 2**20
BF = jnp.bfloat16
F32 = jnp.float32


def swap(value, axis, bit):
    count = lax.axis_size(axis)
    return lax.ppermute(value, axis, [(i, i ^ bit) for i in range(count)])


def pick(array, index, axis=0):
    return lax.dynamic_index_in_dim(array, index, axis, keepdims=False)


def scatter_sum(parts, axis="mp"):
    index = lax.axis_index(axis)
    low, high = index % 2, index // 2
    pairs = parts.reshape((2, 2) + parts.shape[1:])
    kept = pick(pairs, low, 1) + swap(pick(pairs, 1 - low, 1).astype(BF), axis, 1).astype(F32)
    return pick(kept, high, 0) + swap(pick(kept, 1 - high, 0).astype(BF), axis, 2).astype(F32)


def scatter_columns(part):
    rows, width = part.shape
    count = lax.axis_size("mp")
    index = lax.axis_index("mp")
    low, high = index % 2, index // 2
    n = width // count

    def block(array, k):
        return lax.dynamic_slice_in_dim(array, k * n, n, 1)

    sent = jnp.concatenate([block(part, 1 - low), block(part, 3 - low)], axis=1).astype(BF)
    got = swap(sent, "mp", 1).astype(F32)
    mine = block(part, 2 * high + low) + block(got, high)
    other = block(part, 2 * (1 - high) + low) + block(got, 1 - high)
    return mine + swap(other.astype(BF), "mp", 2).astype(F32)


def gather_pairs(block):
    index = lax.axis_index("mp")
    low = index % 2
    across = swap(block, "mp", 2)
    near = swap(block, "mp", 1)
    far = swap(across, "mp", 1)

    def side_by_side(own, other):
        return jnp.concatenate(
            [jnp.where(low == 0, own, other), jnp.where(low == 0, other, own)], axis=1
        )

    return side_by_side(block, near), side_by_side(across, far)


def gathered_product(block, weight, transposed):
    near, far = gather_pairs(block)
    high = lax.axis_index("mp") // 2
    depth = near.shape[1]
    axis, width = (1, weight.shape[0]) if transposed else (0, weight.shape[1])
    size = width // CHUNKS
    first = lax.dynamic_slice_in_dim(weight, high * depth, depth, axis)
    multiply = times_transposed if transposed else dot
    started = multiply(near, first)
    result = []
    for c in range(CHUNKS):
        corner, shape = [c * size] * 2, [size] * 2
        corner[axis], shape[axis] = (1 - high) * depth, depth
        part = lax.dynamic_slice(weight, corner, shape)
        result.append(started[:, c * size : (c + 1) * size] + multiply(far, part))
    return result


def chunked_product(chunks, weight, transposed):
    size = weight.shape[1 if transposed else 0] // CHUNKS
    total = None
    for c, chunk in enumerate(chunks):
        part = lax.slice_in_dim(weight, c * size, (c + 1) * size, axis=1 if transposed else 0)
        product = (times_transposed if transposed else dot)(chunk, part)
        total = product if total is None else total + product
    return total


def split(array):
    return jnp.split(array, CHUNKS, axis=1)


def dot(value, weight):
    return jnp.dot(value, weight, preferred_element_type=F32)


def streamed_kernel(dims, depth, x_ref, w_ref, o_ref):
    o_ref[...] = lax.dot_general(
        x_ref[:, :depth], w_ref[...], dims, preferred_element_type=F32
    ).astype(o_ref.dtype)


def streamed(value, weight, transposed, dtype):
    rows = value.shape[0]
    width, depth = weight.shape if transposed else weight.shape[::-1]
    block = next(b for b in (512, 384, 256, 128) if width % b == 0 and b * depth <= BLOCK)
    if transposed:
        dims, w_spec = (((1,), (1,)), ((), ())), pl.BlockSpec((block, depth), lambda i: (i, 0))
    else:
        dims, w_spec = (((1,), (0,)), ((), ())), pl.BlockSpec((depth, block), lambda i: (0, i))
    return pl.pallas_call(
        functools.partial(streamed_kernel, dims, depth),
        grid=(width // block,),
        in_specs=[pl.BlockSpec(value.shape, lambda i: (0, 0)), w_spec],
        out_specs=pl.BlockSpec((rows, block), lambda i: (0, i)),
        out_shape=jax.ShapeDtypeStruct((rows, width), dtype),
        compiler_params=pltpu.CompilerParams(vmem_limit_bytes=24 * 2**20),
        cost_estimate=pl.CostEstimate(
            flops=2 * rows * width * depth,
            bytes_accessed=2 * (width * depth + rows * depth) + 4 * rows * width,
            transcendentals=0,
        ),
    )(value, weight)


def softmax_rows(query, keys, key_mask):
    scores = jnp.einsum("bqd,brd->bqr", query, keys, preferred_element_type=F32) * HD ** (-0.5)
    scores = jnp.where(key_mask[:, None, :], scores, -1e30)
    raised = jnp.exp(scores - jnp.max(scores, axis=-1, keepdims=True))
    return raised / jnp.sum(raised, axis=-1, keepdims=True)


def attend_back(query, mixed_cot, keys, values, key_mask):
    probs = softmax_rows(query, keys, key_mask)
    prob_cot = jnp.einsum("bqd,brd->bqr", mixed_cot, values, preferred_element_type=F32)
    score_cot = (
        probs * (prob_cot - jnp.sum(prob_cot * probs, axis=-1, keepdims=True)) * HD ** (-0.5)
    ).astype(BF)
    query_cot = jnp.einsum("bqr,brd->bqd", score_cot, keys, preferred_element_type=F32).astype(BF)
    key_cot = jnp.einsum("bqr,bqd->brd", score_cot, query, preferred_element_type=F32)
    value_cot = jnp.einsum("bqr,bqd->brd", probs.astype(BF), mixed_cot, preferred_element_type=F32)
    return query_cot, jnp.concatenate([key_cot, value_cot], axis=-1).astype(BF)


def times_transposed(value, weight):
    return lax.dot_general(value, weight, (((1,), (1,)), ((), ())), preferred_element_type=F32)


def local(
    images,
    ln_gain,
    projector,
    tile_counts,
    assign,
    text,
    text_start,
    w_query,
    w_key,
    w_value,
    w_out,
    gates,
    grad_out,
):
    segments = lax.axis_size("segment")
    groups = lax.axis_size("dp")
    members = lax.axis_size("mp")
    segment_id = lax.axis_index("segment")
    group_id = lax.axis_index("dp")
    member_id = lax.axis_index("mp")
    micro, length, feat_width = text.shape
    rows_img, proj_in = images.shape[1:]
    last_width = ln_gain.shape[0]
    query_width = w_query.shape[2]
    share = rows_img // members
    tokens = micro * length
    first = segment_id == 0
    gate_value = jnp.tanh(gates[0])
    query_weight, out_weight = w_query[0], w_out[0]
    key_weight, value_weight = w_key[0], w_value[0]
    kv_width = key_weight.shape[1]

    own_rows = lax.dynamic_slice_in_dim(images[0], member_id * share, share, 0)
    last_cols = own_rows[:, :last_width].astype(F32)
    center = last_cols - jnp.mean(last_cols, axis=-1, keepdims=True)
    inv_std = lax.rsqrt(jnp.mean(center * center, axis=-1, keepdims=True) + 1e-05)
    normed = center * inv_std
    tile_rows = jnp.concatenate([(normed * ln_gain).astype(BF), own_rows[:, last_width:]], axis=1)

    proj_pad = (-proj_in) % LANES or LANES
    facts = jnp.concatenate([assign, tile_counts]).astype(BF)
    facts = jnp.broadcast_to(facts[None], (share, 2))
    sent = jnp.concatenate(
        [tile_rows, jnp.pad(facts, ((0, 0), (0, proj_pad - 2)))], axis=1
    )
    column = lax.all_gather(sent, "dp", axis=0, tiled=False)
    there = column[:, 0, proj_in].astype(jnp.int32)
    source = jnp.argmax(there // micro == group_id).astype(jnp.int32)
    arrived = lax.all_gather(pick(column, source), ("segment", "mp"), axis=0, tiled=True)
    arrived_facts = arrived.reshape(segments, rows_img, -1)[:, 0, proj_in:].astype(jnp.int32)
    slot_of = arrived_facts[:, 0] % micro
    tiles_of = arrived_facts[:, 1]

    seq_ids = jnp.arange(micro, dtype=jnp.int32)
    chosen = slot_of[None, :] == seq_ids[:, None]
    image_seg = jnp.argmax(chosen, axis=1).astype(jnp.int32)
    counts = jnp.sum(jnp.where(chosen, tiles_of[None, :], 0), axis=1)
    key_mask = jnp.arange(rows_img, dtype=jnp.int32)[None, :] < counts[:, None] * PATCH
    text_live = (
        jnp.arange(length, dtype=jnp.int32)[None, :] >= text_start[:, None]
    ).astype(F32)
    scale = (gate_value * text_live).reshape(tokens, 1)

    text_rows = text.reshape(tokens, feat_width)
    grad_rows = grad_out.reshape(tokens, feat_width)
    out_cot = (scale * grad_rows.astype(F32)).astype(BF)
    early = lax.cond(
        first,
        lambda: streamed(text_rows, query_weight, False, F32),
        lambda: streamed(out_cot, out_weight, True, F32),
    )
    early_sum = scatter_columns(early).astype(BF)

    def heads(array):
        return array.reshape(micro, -1, HD)

    def flat(array):
        return array.reshape(tokens, -1)

    features = streamed(arrived, projector, False, BF)
    key_part = jnp.dot(features, key_weight, preferred_element_type=F32)
    value_part = jnp.dot(features, value_weight, preferred_element_type=F32)
    per = kv_width // members
    parts = jnp.stack([key_part, value_part]).reshape(2, -1, members, per).transpose(2, 0, 1, 3)
    kv_image = scatter_sum(parts).astype(BF).reshape(2, segments, rows_img, per)
    kv = jnp.stack([pick(kv_image, image_seg[i], 1) for i in range(micro)], axis=1)
    keys, values = kv[0], kv[1]

    probs = softmax_rows(heads(early_sum), keys, key_mask)
    mixed = jnp.einsum("bqr,brd->bqd", probs.astype(BF), values, preferred_element_type=F32)
    projected = gathered_product(flat(mixed.astype(BF)), out_weight, False)
    hidden = [
        swap((t.astype(F32) + scale * p).astype(BF), "segment", 1)
        for t, p in zip(split(text_rows), projected)
    ]

    query_late = scatter_columns(chunked_product(hidden, query_weight, False)).astype(BF)
    query_cot, kv_cot_late = attend_back(
        heads(query_late), heads(early_sum), keys, values, key_mask
    )
    query_back = gathered_product(flat(query_cot), query_weight, True)
    cot_late = [(g.astype(F32) + q).astype(BF) for g, q in zip(split(grad_rows), query_back)]
    cot_in = [swap(c, "segment", 1) for c in cot_late]

    out_cot = [(scale * c.astype(F32)).astype(BF) for c in cot_in]
    mixed_cot = scatter_columns(chunked_product(out_cot, out_weight, True)).astype(BF)
    query_cot, kv_cot_early = attend_back(
        heads(early_sum), heads(mixed_cot), keys, values, key_mask
    )
    kv_cot = jnp.where(first, kv_cot_early, kv_cot_late)
    kv_cot = jnp.stack([pick(kv_cot, slot_of[i]) for i in range(segments)])
    kv_all = lax.all_gather(kv_cot.reshape(segments * rows_img, 2 * per), "mp", axis=0)
    near, far = gather_pairs(flat(query_cot))
    high = member_id // 2
    gathered = jnp.concatenate(
        [jnp.where(high == 0, near, far), jnp.where(high == 0, far, near)], axis=1
    )
    query_back = streamed(gathered, query_weight, True, F32)
    cot_early = (jnp.concatenate(cot_in, axis=1).astype(F32) + query_back).astype(BF)
    grads = jnp.where(first, cot_early, jnp.concatenate(cot_late, axis=1))

    key_all = kv_all[:, :, :per].transpose(1, 0, 2).reshape(-1, kv_width)
    value_all = kv_all[:, :, per:].transpose(1, 0, 2).reshape(-1, kv_width)
    feature_cot = (
        times_transposed(key_all, key_weight) + times_transposed(value_all, value_weight)
    ).astype(BF)
    norm_part = streamed(feature_cot, projector, True, F32)
    parts = norm_part.reshape(segments, members, share, proj_in).transpose(1, 0, 2, 3)
    summed = scatter_sum(parts)
    returned = pick(summed, segment_id) + swap(
        pick(summed, 1 - segment_id).astype(BF), "segment", 1
    ).astype(F32)
    back_pad = (-proj_in) % BACK_LANES
    column = lax.all_gather(
        jnp.pad(returned.astype(BF), ((0, 0), (0, back_pad))), "dp", axis=0, tiled=False
    )
    norm_cot = pick(column, assign[0] // micro)[:, :proj_in].astype(F32)
    scaled = norm_cot[:, :last_width] * ln_gain
    last_grad = inv_std * (
        scaled
        - jnp.mean(scaled, axis=-1, keepdims=True)
        - normed * jnp.mean(scaled * normed, axis=-1, keepdims=True)
    )
    result = jnp.concatenate([last_grad, norm_cot[:, last_width:]], axis=1).astype(BF)
    result = lax.all_gather(result, "mp", axis=0, tiled=True)
    return (grads.reshape(1, micro, length, feat_width), result[None])


def solution(mesh):
    return jax.shard_map(
        local,
        mesh=mesh,
        in_specs=(
            P(("segment", "dp"), None, None),
            P(),
            P(None, "mp"),
            P(("segment", "dp")),
            P(("segment", "dp")),
            P("dp", None, "mp"),
            P("dp"),
            P("segment", "mp", None),
            P("segment", "mp", None),
            P("segment", "mp", None),
            P("segment", None, "mp"),
            P("segment"),
            P("dp", None, "mp"),
        ),
        out_specs=(P("segment", "dp", None, "mp"), P(("segment", "dp"), None, None)),
        check_vma=False,
    )
```

profile of v0, /device:TPU:0, one launch (start us, length us, event | category | flops | bytes accessed | tf_op | source)
XLA Modules:
  0.0 326.8 jit_solution(11915513535138633181)
XLA Ops:
  7.3 1.1 copy-done
  11.0 23.9 %all-gather = bf16[128,3968]{1,0:T(8,128)(2,1)S(1)} all-gather(bf16[32,3968]{1,0:T(8,128)(2,1)S(1)} %maximum_maximum_fusion), channel_id=2, replica_groups=mesh['segment'=2,'dp'=4,'mp'=4] {'dp'}, dimensions={0}, use_global_device_ids=true | all-gather | bytes 1269760 | tf_op jit(solution)/shard_map/all_gather | solution.py:203
  40.3 9.4 %conditional.1 = (f32[128,4096]{1,0:T(8,128)S(1)}) conditional(s32[]{:T(128)} %convert_element_type.206, (bf16[128,2048]{1,0:T(8,128)(2,1)}, bf16[4096,2048]{1,0:T(8,128)(2,1)}) %tuple.49, (bf16[128,2048]{1,0:T(8,128)(2,1)S(1)}, bf16[2048,4096]{1,0:T(8,128)(2,1)}) %tuple.50), branch_computations={%region_4.5_spmd, %region_5.6_spmd} | conditional | flops 2147483648 | bytes 19398664 | solution.py:224
  40.3 9.4 %branch_1_fun.1 = f32[128,4096]{1,0:T(8,128)S(1)} custom-call(bf16[128,2048]{1,0:T(8,128)(2,1)S(1)} %get-tuple-element.13.x_ref, bf16[2048,4096]{1,0:T(8,128)(2,1)} %get-tuple-element.14.w_ref), custom_call_target="tpu_custom_call" | custom-call | flops 2147483648 | bytes 19398656 | tf_op jit(solution)/shard_map/cond/branch_1_fun/pallas_call | solution.py:119
  50.7 2.2 collective-permute-done
  53.0 1.1 convert_element_type.209
  56.0 1.6 collective-permute-start.1
  57.5 4.1 %copy.92 = bf16[512,2048]{1,0:T(8,128)(2,1)} copy(bf16[512,2048]{0,1:T(8,128)(2,1)} %bitcast.194) | data formatting | bytes 4194304 | tf_op jit(solution)/shard_map/dot_general | solution.py:239
  61.7 2.5 copy.91
  64.1 5.9 %collective-permute-done.1 = bf16[128,1024]{1,0:T(8,128)(2,1)S(1)} collective-permute-done((bf16[128,1024]{1,0:T(8,128)(2,1)}, bf16[128,1024]{1,0:T(8,128)(2,1)S(1)}, u32[]{:S(2)}, u32[]{:S(2)}) %collective-permute-start.1) | collective-permute-done | bytes 262176 | tf_op jit(solution)/shard_map/ppermute | solution.py:22
  70.0 2.0 add_convert_fusion.5
  73.9 5.5 %copy-done.2 = bf16[3840,2048]{1,0:T(8,128)(2,1)S(1)} copy-done((bf16[3840,2048]{1,0:T(8,128)(2,1)S(1)}, bf16[3840,2048]{1,0:T(8,128)(2,1)}, u32[]{:S(2)}) %copy-start.2) | copy-done | bytes 15728664
  79.4 1.6 copy-done.4
  81.0 7.9 %shard_map.140 = bf16[256,2048]{1,0:T(8,128)(2,1)S(1)} custom-call(bf16[256,3968]{1,0:T(8,128)(2,1)S(1)} %bitcast.183, bf16[3840,2048]{1,0:T(8,128)(2,1)S(1)} %copy-done.2), custom_call_target="tpu_custom_call" | custom-call | flops 4026531840 | bytes 19791872 | tf_op jit(solution)/shard_map/pallas_call | solution.py:119
  98.6 1.2 bitcast_add_fusion.2
  100.5 5.1 %collective-permute-done.3 = bf16[2,256,128]{2,1,0:T(8,128)(2,1)S(1)} collective-permute-done((bf16[2,256,128]{2,1,0:T(8,128)(2,1)S(1)}, bf16[2,256,128]{2,1,0:T(8,128)(2,1)S(1)}, u32[]{:S(2)}, u32[]{:S(2)}) %collective-permute-start.3) | collective-permute-done | bytes 131104 | tf_op jit(solution)/shard_map/ppermute | solution.py:22
  105.6 1.1 fusion.185
  106.8 1.2 convolution_convert_fusion.2
  108.0 1.8 reshape.199
  110.3 7.5 %collective-permute-done.5 = bf16[128,1024]{1,0:T(8,128)(2,1)} collective-permute-done((bf16[128,1024]{1,0:T(8,128)(2,1)}, bf16[128,1024]{1,0:T(8,128)(2,1)}, u32[]{:S(2)}, u32[]{:S(2)}) %collective-permute-start.5) | collective-permute-done | bytes 262176 | tf_op jit(solution)/shard_map/ppermute | solution.py:22
  117.8 1.1 broadcast_select_fusion.13
  118.9 4.8 %fusion.14 = f32[128,2048]{1,0:T(8,128)S(1)} fusion(bf16[1,4096,2048]{2,1,0:T(8,128)(2,1)} %param.25, s32[]{:T(128)S(6)} %select_n.264, bf16[128,1024]{1,0:T(8,128)(2,1)S(1)} %get-tuple-element.44, bf16[128,1024]{1,0:T(8,128)(2,1)S(1)} %get-tuple-element.43), kind=kOutput, calls=%fused_computation.14 | convolution fusion | flops 1074790400 | bytes 9961476 | tf_op jit(solution)/shard_map/dot_general | solution.py:102
  124.8 3.0 fusion.86
  127.8 1.8 collective-permute-start.8
  129.6 3.0 fusion.89
  133.2 3.8 %collective-permute-done.8 = bf16[128,1024]{1,0:T(8,128)(2,1)S(1)} collective-permute-done((bf16[128,1024]{1,0:T(8,128)(2,1)S(1)}, bf16[128,1024]{1,0:T(8,128)(2,1)S(1)}, u32[]{:S(2)}, u32[]{:S(2)}) %collective-permute-start.8) | collective-permute-done | bytes 262176 | tf_op jit(solution)/shard_map/ppermute | solution.py:22
  137.0 4.7 %fusion.10 = f32[128,4096]{1,0:T(8,128)S(1)} fusion(bf16[128,1024]{1,0:T(8,128)(2,1)S(1)} %collective-permute-done.8, bf16[1,2048,4096]{2,1,0:T(8,128)(2,1)} %param.22), kind=kOutput, calls=%fused_computation.10 | convolution fusion | flops 1073741824 | bytes 10747904 | tf_op jit(solution)/shard_map/dot_general | solution.py:102
  142.2 1.3 fusion.20
  143.8 1.9 collective-permute-done.9
  147.5 6.8 %collective-permute-done.10 = bf16[128,1024]{1,0:T(8,128)(2,1)S(1)} collective-permute-done((bf16[128,1024]{1,0:T(8,128)(2,1)S(1)}, bf16[128,1024]{1,0:T(8,128)(2,1)S(1)}, u32[]{:S(2)}, u32[]{:S(2)}) %collective-permute-start.10) | collective-permute-done | bytes 262176 | tf_op jit(solution)/shard_map/ppermute | solution.py:22
  154.5 1.1 fusion.186
  155.6 2.7 convolution_convert_fusion.1
  158.4 1.1 reshape.201
  160.1 7.0 %collective-permute-done.12 = bf16[128,1024]{1,0:T(8,128)(2,1)S(1)} collective-permute-done((bf16[128,1024]{1,0:T(8,128)(2,1)S(1)}, bf16[128,1024]{1,0:T(8,128)(2,1)S(1)}, u32[]{:S(2)}, u32[]{:S(2)}) %collective-permute-start.12) | collective-permute-done | bytes 262176 | tf_op jit(solution)/shard_map/ppermute | solution.py:22
  167.1 6.4 %fusion.8 = f32[128,2048]{1,0:T(8,128)S(1)} fusion(bf16[1,2048,4096]{2,1,0:T(8,128)(2,1)} %param.22, s32[]{:T(128)S(6)} %select_n.264, bf16[128,1024]{1,0:T(8,128)(2,1)S(1)} %get-tuple-element.40, bf16[128,1024]{1,0:T(8,128)(2,1)S(1)} %get-tuple-element.39), kind=kOutput, calls=%fused_computation.8 | convolution fusion | flops 1074790400 | bytes 9961476 | tf_op jit(solution)/shard_map/dot_general | solution.py:154
  173.6 3.8 %fusion.92 = bf16[128,1024]{1,0:T(8,128)(2,1)S(1)} fusion(bf16[1,2048,4096]{2,1,0:T(8,128)(2,1)} %param.22, s32[]{:T(128)S(6)} %select_n.267, f32[128,2048]{1,0:T(8,128)S(1)} %fusion.8, bf16[128,1024]{1,0:T(8,128)(2,1)S(1)} %get-tuple-element.38, bf16[128,1024]{1,0:T(8,128)(2,1)S(1)} %get-tuple-element.37, bf16[128,2048]{1,0:T(8,128)(2,1)S(1)} %bitcast.201), kind=kOutput, calls=%fused_computation.71 | convolution fusion | flops 538443776 | bytes 5767172 | tf_op jit(solution)/shard_map/dot_general | solution.py:154
  177.4 1.8 collective-permute-start.15
  179.2 4.0 %fusion.95 = bf16[128,1024]{1,0:T(8,128)(2,1)S(1)} fusion(bf16[1,2048,4096]{2,1,0:T(8,128)(2,1)} %param.22, s32[]{:T(128)S(6)} %select_n.267, f32[128,2048]{1,0:T(8,128)S(1)} %fusion.8, bf16[128,1024]{1,0:T(8,128)(2,1)S(1)} %get-tuple-element.38, bf16[128,1024]{1,0:T(8,128)(2,1)S(1)} %get-tuple-element.37, bf16[128,2048]{1,0:T(8,128)(2,1)S(1)} %bitcast.202), kind=kOutput, calls=%fused_computation.72 | convolution fusion | flops 538443776 | bytes 5767172 | tf_op jit(solution)/shard_map/dot_general | solution.py:154
  183.9 2.4 collective-permute-done.15
  186.3 6.4 %fusion.4 = f32[128,4096]{1,0:T(8,128)S(1)} fusion(bf16[4096,2048]{1,0:T(8,128)(2,1)} %bitcast.189, bf16[128,1024]{1,0:T(8,128)(2,1)S(1)} %collective-permute-done.15, f32[128]{0:T(128)S(1)} %mul.179), kind=kOutput, calls=%fused_computation.4 | convolution fusion | flops 1074135040 | bytes 10748416 | tf_op jit(solution)/shard_map/dot_general | solution.py:154
  193.4 2.9 fusion.23
  196.3 1.3 copy-done.6
  204.0 1.2 add_convert_fusion.2
  205.7 2.1 convolution_convert_fusion.4
  208.3 5.7 %collective-permute-done.17 = bf16[128,1024]{1,0:T(8,128)(2,1)} collective-permute-done((bf16[128,1024]{1,0:T(8,128)(2,1)S(1)}, bf16[128,1024]{1,0:T(8,128)(2,1)}, u32[]{:S(2)}, u32[]{:S(2)}) %collective-permute-start.17) | collective-permute-done | bytes 262176 | tf_op jit(solution)/shard_map/ppermute | solution.py:22
  214.0 1.4 add_convert_fusion.1
  217.0 2.2 convolution_convert_fusion.6
  219.5 6.7 %all_gather.24 = bf16[4,256,256]{2,1,0:T(8,128)(2,1)S(1)} all-gather(bf16[1,256,256]{2,1,0:T(8,128)(2,1)S(1)} %bitcast.210), channel_id=1, replica_groups=mesh['segment'=2,'dp'=4,'mp'=4] {'mp'}, dimensions={0}, use_global_device_ids=true | all-gather | bytes 655360 | tf_op jit(solution)/shard_map/all_gather | solution.py:269
  227.0 1.1 copy.94
  228.0 2.1 fusion.40
  230.3 3.0 fusion.38.x_ref
  233.3 5.5 %copy-done.3 = bf16[3840,2048]{1,0:T(8,128)(2,1)S(1)} copy-done((bf16[3840,2048]{1,0:T(8,128)(2,1)S(1)}, bf16[3840,2048]{1,0:T(8,128)(2,1)}, u32[]{:S(2)}) %copy-start.3) | copy-done | bytes 15728664
  238.8 7.5 %shard_map.142 = f32[256,3840]{1,0:T(8,128)S(1)} custom-call(bf16[256,2048]{1,0:T(8,128)(2,1)S(1)} %fusion.38.x_ref, bf16[3840,2048]{1,0:T(8,128)(2,1)S(1)} %copy-done.3), custom_call_target="tpu_custom_call" | custom-call | flops 4026531840 | bytes 20709376 | tf_op jit(solution)/shard_map/pallas_call | solution.py:119
  246.8 2.2 collective-permute-done.21
  249.3 1.1 collective-permute-start.22
  250.3 2.2 convolution_convert_fusion
  254.4 14.1 %collective-permute-done.19 = bf16[128,1024]{1,0:T(8,128)(2,1)} collective-permute-done((bf16[128,1024]{1,0:T(8,128)(2,1)}, bf16[128,1024]{1,0:T(8,128)(2,1)}, u32[]{:S(2)}, u32[]{:S(2)}) %collective-permute-start.19) | collective-permute-done | bytes 262176 | tf_op jit(solution)/shard_map/ppermute | solution.py:22
  268.5 1.1 bitcast_add_fusion.1
  269.7 2.1 collective-permute-start.23
  272.8 5.6 %collective-permute-done.23 = bf16[32,3840]{1,0:T(8,128)(2,1)S(1)} collective-permute-done((bf16[32,3840]{1,0:T(8,128)(2,1)S(1)}, bf16[32,3840]{1,0:T(8,128)(2,1)S(1)}, u32[]{:S(2)}, u32[]{:S(2)}) %collective-permute-start.23) | collective-permute-done | bytes 245792 | tf_op jit(solution)/shard_map/ppermute | solution.py:22
  279.2 1.1 broadcast_select_fusion.3
  280.6 11.2 %shard_map.141 = f32[128,2048]{1,0:T(8,128)S(1)} custom-call(bf16[128,4096]{1,0:T(8,128)(2,1)S(1)} %pad_maximum_fusion.1.x_ref, bf16[2048,4096]{1,0:T(8,128)(2,1)} %bitcast.185), custom_call_target="tpu_custom_call" | custom-call | flops 2147483648 | bytes 18874368 | tf_op jit(solution)/shard_map/pallas_call | solution.py:119
  292.8 15.2 %all-gather.8.cloned.1.call-done = bf16[128,4096]{1,0:T(8,128)(2,1)} async-done(((bf16[32,4096]{1,0:T(8,128)(2,1)}), bf16[128,4096]{1,0:T(8,128)(2,1)}) %all-gather.8.cloned.1.call-update) | async-done | bytes 1048592 | tf_op jit(solution)/shard_map/all_gather | solution.py:291
  309.4 9.7 %all_gather.27 = bf16[128,3840]{1,0:T(8,128)(2,1)S(1)} all-gather(bf16[32,3840]{1,0:T(8,128)(2,1)S(1)} %pad_maximum_fusion.13), channel_id=1, replica_groups=mesh['segment'=2,'dp'=4,'mp'=4] {'mp'}, dimensions={0}, use_global_device_ids=true | all-gather | bytes 1228800 | tf_op jit(solution)/shard_map/all_gather | solution.py:302
  (184 shorter events, 36.9 us)
Async XLA Ops:
  7.2 1.2 copy-start
  7.2 32.0 %copy-start.27 = (s32[2]{0:T(128)S(1)}, s32[2]{0:T(128)}, u32[]{:S(2)}) copy-start(s32[2]{0:T(128)} %param.21) | copy-start | bytes 28
  7.2 32.1 %copy-start.12 = (bf16[2,64,2048]{2,1,0:T(8,128)(2,1)S(1)}, bf16[2,64,2048]{2,1,0:T(8,128)(2,1)}, u32[]{:S(2)}) copy-start(bf16[2,64,2048]{2,1,0:T(8,128)(2,1)} %param.27) | copy-start | bytes 1572868
  7.2 65.9 %all-gather.6.cloned.1.call-start = ((), (), s32[]{:S(2)}) async-start(), calls=%async_computation | async-start | bytes 2285568 | tf_op jit(solution)/shard_map/all_gather | solution.py:206
  8.4 31.9 %copy-start.11 = (bf16[2,64,2048]{2,1,0:T(8,128)(2,1)S(1)}, bf16[2,64,2048]{2,1,0:T(8,128)(2,1)}, u32[]{:S(2)}) copy-start(bf16[2,64,2048]{2,1,0:T(8,128)(2,1)} %param.20) | copy-start | bytes 1572868
  38.4 269.7 %all-gather.8.cloned.1.call-start = ((), (), s32[]{:S(2)}) async-start(), calls=%async_computation.1 | async-start | bytes 1310720 | tf_op jit(solution)/shard_map/all_gather | solution.py:291
  49.7 6.3 %copy-start.7 = (f32[128,4096]{1,0:T(8,128)}, f32[128,4096]{1,0:T(8,128)S(1)}, u32[]{:S(2)}) copy-start(f32[128,4096]{1,0:T(8,128)S(1)} %get-tuple-element.63) | copy-start | bytes 6291460
  50.7 2.3 collective-permute-start
  54.1 1.1 copy-start.8
  56.0 14.0 %collective-permute-start.1 = (bf16[128,1024]{1,0:T(8,128)(2,1)}, bf16[128,1024]{1,0:T(8,128)(2,1)S(1)}, u32[]{:S(2)}, u32[]{:S(2)}) collective-permute-start(bf16[128,1024]{1,0:T(8,128)(2,1)} %add_convert_fusion.6), channel_id=1, source_target_pairs={{0,2},{1,3},{2,0},{3,1},{4,6},{5,7},{6,4},{7,5},{8,10},{9,11},{10,... | collective-permute-start | bytes 786440 | tf_op jit(solution)/shard_map/ppermute | solution.py:22
  57.5 4.1 %copy-start.5 = (bf16[1,2048,512]{2,1,0:T(8,128)(2,1)S(1)}, bf16[1,2048,512]{2,1,0:T(8,128)(2,1)}, u32[]{:S(2)}) copy-start(bf16[1,2048,512]{2,1,0:T(8,128)(2,1)} %param.23) | copy-start | bytes 6291460
  73.9 5.5 %copy-start.2 = (bf16[3840,2048]{1,0:T(8,128)(2,1)S(1)}, bf16[3840,2048]{1,0:T(8,128)(2,1)}, u32[]{:S(2)}) copy-start(bf16[3840,2048]{1,0:T(8,128)(2,1)} %w_ref.3) | copy-start | bytes 47185924
  79.4 1.6 copy-start.4
  81.0 7.9 %copy-start.15 = (bf16[512,2048]{1,0:T(8,128)(2,1)S(1)}, bf16[512,2048]{1,0:T(8,128)(2,1)}, u32[]{:S(2)}) copy-start(bf16[512,2048]{1,0:T(8,128)(2,1)} %copy.92) | copy-start | bytes 6291460
  88.9 1.6 copy-start.14
  91.4 1.0 copy-start.10
  93.2 5.4 %collective-permute-start.2 = (bf16[2,2,256,128]{3,2,0,1:T(8,128)(2,1)}, bf16[2,2,256,128]{3,2,0,1:T(8,128)(2,1)}, u32[]{:S(2)}, u32[]{:S(2)}) collective-permute-start(bf16[2,2,256,128]{3,2,0,1:T(8,128)(2,1)} %fusion.118), channel_id=1, source_target_pairs={{0,1},{1,0},{2,3},{3,2},{4,5},{5,4},{6,7},{7,6},{8,9},{9,8},{10,11... | collective-permute-start | bytes 786440 | tf_op jit(solution)/shard_map/ppermute | solution.py:22
  99.8 5.8 %collective-permute-start.3 = (bf16[2,256,128]{2,1,0:T(8,128)(2,1)S(1)}, bf16[2,256,128]{2,1,0:T(8,128)(2,1)S(1)}, u32[]{:S(2)}, u32[]{:S(2)}) collective-permute-start(bf16[2,256,128]{2,1,0:T(8,128)(2,1)S(1)} %fusion.140), channel_id=1, source_target_pairs={{0,2},{1,3},{2,0},{3,1},{4,6},{5,7},{6,4},{7,5},{8,10},{9,11},{10,... | collective-permute-start | bytes 393224 | tf_op jit(solution)/shard_map/ppermute | solution.py:22
  109.8 8.1 %collective-permute-start.5 = (bf16[128,1024]{1,0:T(8,128)(2,1)}, bf16[128,1024]{1,0:T(8,128)(2,1)}, u32[]{:S(2)}, u32[]{:S(2)}) collective-permute-start(bf16[128,1024]{1,0:T(8,128)(2,1)} %reshape.199), channel_id=1, source_target_pairs={{0,2},{1,3},{2,0},{3,1},{4,6},{5,7},{6,4},{7,5},{8,10},{9,11},{10,... | collective-permute-start | bytes 786440 | tf_op jit(solution)/shard_map/ppermute | solution.py:22
  110.3 7.5 %collective-permute-start.4 = (bf16[128,1024]{1,0:T(8,128)(2,1)}, bf16[128,1024]{1,0:T(8,128)(2,1)}, u32[]{:S(2)}, u32[]{:S(2)}) collective-permute-start(bf16[128,1024]{1,0:T(8,128)(2,1)} %reshape.199), channel_id=1, source_target_pairs={{0,1},{1,0},{2,3},{3,2},{4,5},{5,4},{6,7},{7,6},{8,9},{9,8},{10,11... | collective-permute-start | bytes 786440 | tf_op jit(solution)/shard_map/ppermute | solution.py:22
  117.8 5.9 %collective-permute-start.6 = (bf16[128,1024]{1,0:T(8,128)(2,1)}, bf16[128,1024]{1,0:T(8,128)(2,1)S(1)}, u32[]{:S(2)}, u32[]{:S(2)}) collective-permute-start(bf16[128,1024]{1,0:T(8,128)(2,1)} %collective-permute-done.5), channel_id=1, source_target_pairs={{0,1},{1,0},{2,3},{3,2},{4,5},{5,4},{6,7},{7,6},{8,9},{9,8},{10,11... | collective-permute-start | bytes 786440 | tf_op jit(solution)/shard_map/ppermute | solution.py:22
  118.9 23.3 %slice-start = ((s8[16777216]{0:T(1024)(128)(4,1)}), s8[4194304]{0:T(1024)(128)(4,1)S(1)}, s32[]{:S(2)}) async-start(s8[16777216]{0:T(1024)(128)(4,1)} %bitcast.186), calls=%async_computation.2 | async-start | bytes 8388608
  118.9 23.3 %slice-start.1 = ((s8[16777216]{0:T(1024)(128)(4,1)}), s8[4194304]{0:T(1024)(128)(4,1)S(1)}, s32[]{:S(2)}) async-start(s8[16777216]{0:T(1024)(128)(4,1)} %bitcast.186), calls=%async_computation.3 | async-start | bytes 8388608
  127.8 14.4 %slice-start.2 = ((s8[16777216]{0:T(1024)(128)(4,1)}), s8[4194304]{0:T(1024)(128)(4,1)S(1)}, s32[]{:S(2)}) async-start(s8[16777216]{0:T(1024)(128)(4,1)} %bitcast.186), calls=%async_computation.4 | async-start | bytes 8388608
  127.8 9.2 %collective-permute-start.8 = (bf16[128,1024]{1,0:T(8,128)(2,1)S(1)}, bf16[128,1024]{1,0:T(8,128)(2,1)S(1)}, u32[]{:S(2)}, u32[]{:S(2)}) collective-permute-start(bf16[128,1024]{1,0:T(8,128)(2,1)S(1)} %fusion.86), channel_id=1, source_target_pairs={{0,16},{16,0},{1,17},{17,1},{2,18},{18,2},{3,19},{19,3},{4,20},{20... | collective-permute-start | bytes 786440 | tf_op jit(solution)/shard_map/ppermute | solution.py:22
  132.6 9.6 %slice-start.3 = ((s8[16777216]{0:T(1024)(128)(4,1)}), s8[4194304]{0:T(1024)(128)(4,1)S(1)}, s32[]{:S(2)}) async-start(s8[16777216]{0:T(1024)(128)(4,1)} %bitcast.186), calls=%async_computation.5 | async-start | bytes 8388608
  132.6 9.6 %collective-permute-start.7 = (bf16[128,1024]{1,0:T(8,128)(2,1)S(1)}, bf16[128,1024]{1,0:T(8,128)(2,1)S(1)}, u32[]{:S(2)}, u32[]{:S(2)}) collective-permute-start(bf16[128,1024]{1,0:T(8,128)(2,1)S(1)} %fusion.89), channel_id=1, source_target_pairs={{0,16},{16,0},{1,17},{17,1},{2,18},{18,2},{3,19},{19,3},{4,20},{20... | collective-permute-start | bytes 786440 | tf_op jit(solution)/shard_map/ppermute | solution.py:22
  143.7 2.0 collective-permute-start.9
  145.9 8.4 %collective-permute-start.10 = (bf16[128,1024]{1,0:T(8,128)(2,1)S(1)}, bf16[128,1024]{1,0:T(8,128)(2,1)S(1)}, u32[]{:S(2)}, u32[]{:S(2)}) collective-permute-start(bf16[128,1024]{1,0:T(8,128)(2,1)S(1)} %add_convert_fusion.4), channel_id=1, source_target_pairs={{0,2},{1,3},{2,0},{3,1},{4,6},{5,7},{6,4},{7,5},{8,10},{9,11},{10,... | collective-permute-start | bytes 786440 | tf_op jit(solution)/shard_map/ppermute | solution.py:22
  154.5 4.9 %copy-start.22 = (bf16[2,512,128]{2,1,0:T(8,128)(2,1)}, bf16[2,512,128]{2,1,0:T(8,128)(2,1)S(1)}, u32[]{:S(2)}) copy-start(bf16[2,512,128]{2,1,0:T(8,128)(2,1)S(1)} %reshape.200) | copy-start | bytes 786436
  159.4 7.6 %collective-permute-start.12 = (bf16[128,1024]{1,0:T(8,128)(2,1)S(1)}, bf16[128,1024]{1,0:T(8,128)(2,1)S(1)}, u32[]{:S(2)}, u32[]{:S(2)}) collective-permute-start(bf16[128,1024]{1,0:T(8,128)(2,1)S(1)} %reshape.201), channel_id=1, source_target_pairs={{0,2},{1,3},{2,0},{3,1},{4,6},{5,7},{6,4},{7,5},{8,10},{9,11},{10,... | collective-permute-start | bytes 786440 | tf_op jit(solution)/shard_map/ppermute | solution.py:22
  160.1 7.0 %collective-permute-start.11 = (bf16[128,1024]{1,0:T(8,128)(2,1)S(1)}, bf16[128,1024]{1,0:T(8,128)(2,1)S(1)}, u32[]{:S(2)}, u32[]{:S(2)}) collective-permute-start(bf16[128,1024]{1,0:T(8,128)(2,1)S(1)} %reshape.201), channel_id=1, source_target_pairs={{0,1},{1,0},{2,3},{3,2},{4,5},{5,4},{6,7},{7,6},{8,9},{9,8},{10,11... | collective-permute-start | bytes 786440 | tf_op jit(solution)/shard_map/ppermute | solution.py:22
  167.0 6.5 %collective-permute-start.13 = (bf16[128,1024]{1,0:T(8,128)(2,1)S(1)}, bf16[128,1024]{1,0:T(8,128)(2,1)S(1)}, u32[]{:S(2)}, u32[]{:S(2)}) collective-permute-start(bf16[128,1024]{1,0:T(8,128)(2,1)S(1)} %collective-permute-done.12), channel_id=1, source_target_pairs={{0,1},{1,0},{2,3},{3,2},{4,5},{5,4},{6,7},{7,6},{8,9},{9,8},{10,11... | collective-permute-start | bytes 786440 | tf_op jit(solution)/shard_map/ppermute | solution.py:22
  167.1 6.6 %copy-start.13 = (bf16[2,64,2048]{2,1,0:T(8,128)(2,1)S(1)}, bf16[2,64,2048]{2,1,0:T(8,128)(2,1)}, u32[]{:S(2)}) copy-start(bf16[2,64,2048]{2,1,0:T(8,128)(2,1)} %param.27) | copy-start | bytes 1572868
  167.1 26.3 %slice-start.4 = ((s8[16777216]{0:T(1024)(128)(4,1)}), s8[4194304]{0:T(1024)(128)(4,1)S(1)}, s32[]{:S(2)}) async-start(s8[16777216]{0:T(1024)(128)(4,1)} %bitcast.190), calls=%async_computation.6 | async-start | bytes 8388608
  167.1 26.3 %slice-start.5 = ((s8[16777216]{0:T(1024)(128)(4,1)}), s8[4194304]{0:T(1024)(128)(4,1)S(1)}, s32[]{:S(2)}) async-start(s8[16777216]{0:T(1024)(128)(4,1)} %bitcast.190), calls=%async_computation.7 | async-start | bytes 8388608
  177.4 5.8 %copy-start.16 = (bf16[128,1024]{1,0:T(8,128)(2,1)}, bf16[128,1024]{1,0:T(8,128)(2,1)S(1)}, u32[]{:S(2)}) copy-start(bf16[128,1024]{1,0:T(8,128)(2,1)S(1)} %fusion.92) | copy-start | bytes 786436
  177.4 16.0 %slice-start.6 = ((s8[16777216]{0:T(1024)(128)(4,1)}), s8[4194304]{0:T(1024)(128)(4,1)S(1)}, s32[]{:S(2)}) async-start(s8[16777216]{0:T(1024)(128)(4,1)} %bitcast.190), calls=%async_computation.8 | async-start | bytes 8388608
  177.4 8.8 %collective-permute-start.15 = (bf16[128,1024]{1,0:T(8,128)(2,1)S(1)}, bf16[128,1024]{1,0:T(8,128)(2,1)S(1)}, u32[]{:S(2)}, u32[]{:S(2)}) collective-permute-start(bf16[128,1024]{1,0:T(8,128)(2,1)S(1)} %fusion.92), channel_id=1, source_target_pairs={{0,16},{16,0},{1,17},{17,1},{2,18},{18,2},{3,19},{19,3},{4,20},{20... | collective-permute-start | bytes 786440 | tf_op jit(solution)/shard_map/ppermute | solution.py:22
  183.2 9.5 %copy-start.18 = (bf16[128,1024]{1,0:T(8,128)(2,1)}, bf16[128,1024]{1,0:T(8,128)(2,1)S(1)}, u32[]{:S(2)}) copy-start(bf16[128,1024]{1,0:T(8,128)(2,1)S(1)} %fusion.95) | copy-start | bytes 786436
  183.2 10.2 %slice-start.7 = ((s8[16777216]{0:T(1024)(128)(4,1)}), s8[4194304]{0:T(1024)(128)(4,1)S(1)}, s32[]{:S(2)}) async-start(s8[16777216]{0:T(1024)(128)(4,1)} %bitcast.190), calls=%async_computation.9 | async-start | bytes 8388608
  183.2 9.5 %collective-permute-start.14 = (bf16[128,1024]{1,0:T(8,128)(2,1)S(1)}, bf16[128,1024]{1,0:T(8,128)(2,1)S(1)}, u32[]{:S(2)}, u32[]{:S(2)}) collective-permute-start(bf16[128,1024]{1,0:T(8,128)(2,1)S(1)} %fusion.95), channel_id=1, source_target_pairs={{0,16},{16,0},{1,17},{17,1},{2,18},{18,2},{3,19},{19,3},{4,20},{20... | collective-permute-start | bytes 786440 | tf_op jit(solution)/shard_map/ppermute | solution.py:22
  186.3 6.4 %copy-start.24 = (bf16[128,1024]{1,0:T(8,128)(2,1)}, bf16[128,1024]{1,0:T(8,128)(2,1)S(1)}, u32[]{:S(2)}) copy-start(bf16[128,1024]{1,0:T(8,128)(2,1)S(1)} %collective-permute-done.15) | copy-start | bytes 786436
  192.7 0.7 copy-start.20
  196.3 1.3 copy-start.6
  198.5 4.3 %collective-permute-start.16 = (bf16[128,2048]{1,0:T(8,128)(2,1)}, bf16[128,2048]{1,0:T(8,128)(2,1)S(1)}, u32[]{:S(2)}, u32[]{:S(2)}) collective-permute-start(bf16[128,2048]{1,0:T(8,128)(2,1)} %pad_maximum_fusion.6), channel_id=1, source_target_pairs={{0,1},{1,0},{2,3},{3,2},{4,5},{5,4},{6,7},{7,6},{8,9},{9,8},{10,11... | collective-permute-start | bytes 1572872 | tf_op jit(solution)/shard_map/ppermute | solution.py:22
  203.0 1.0 copy-start.9
  204.0 3.9 %copy-start.23 = (bf16[2,512,128]{2,1,0:T(8,128)(2,1)S(1)}, bf16[2,512,128]{2,1,0:T(8,128)(2,1)}, u32[]{:S(2)}) copy-start(bf16[2,512,128]{2,1,0:T(8,128)(2,1)} %copy-done.22) | copy-start | bytes 786436
  205.1 8.9 %collective-permute-start.17 = (bf16[128,1024]{1,0:T(8,128)(2,1)S(1)}, bf16[128,1024]{1,0:T(8,128)(2,1)}, u32[]{:S(2)}, u32[]{:S(2)}) collective-permute-start(bf16[128,1024]{1,0:T(8,128)(2,1)S(1)} %add_convert_fusion.2), channel_id=1, source_target_pairs={{0,2},{1,3},{2,0},{3,1},{4,6},{5,7},{6,4},{7,5},{8,10},{9,11},{10,... | collective-permute-start | bytes 786440 | tf_op jit(solution)/shard_map/ppermute | solution.py:22
  233.3 5.5 %copy-start.3 = (bf16[3840,2048]{1,0:T(8,128)(2,1)S(1)}, bf16[3840,2048]{1,0:T(8,128)(2,1)}, u32[]{:S(2)}) copy-start(bf16[3840,2048]{1,0:T(8,128)(2,1)} %w_ref.3) | copy-start | bytes 47185924
  246.4 2.6 collective-permute-start.21
  249.3 19.3 %collective-permute-start.22 = (bf16[2,32,3840]{2,1,0:T(8,128)(2,1)S(1)}, bf16[2,32,3840]{2,1,0:T(8,128)(2,1)}, u32[]{:S(2)}, u32[]{:S(2)}) collective-permute-start(bf16[2,32,3840]{2,1,0:T(8,128)(2,1)S(1)} %fusion.116), channel_id=1, source_target_pairs={{0,2},{1,3},{2,0},{3,1},{4,6},{5,7},{6,4},{7,5},{8,10},{9,11},{10,... | collective-permute-start | bytes 1474568 | tf_op jit(solution)/shard_map/ppermute | solution.py:22
  253.4 15.1 %collective-permute-start.19 = (bf16[128,1024]{1,0:T(8,128)(2,1)}, bf16[128,1024]{1,0:T(8,128)(2,1)}, u32[]{:S(2)}, u32[]{:S(2)}) collective-permute-start(bf16[128,1024]{1,0:T(8,128)(2,1)} %reshape.203), channel_id=1, source_target_pairs={{0,2},{1,3},{2,0},{3,1},{4,6},{5,7},{6,4},{7,5},{8,10},{9,11},{10,... | collective-permute-start | bytes 786440 | tf_op jit(solution)/shard_map/ppermute | solution.py:22
  254.4 17.4 %collective-permute-start.18 = (bf16[128,1024]{1,0:T(8,128)(2,1)}, bf16[128,1024]{1,0:T(8,128)(2,1)S(1)}, u32[]{:S(2)}, u32[]{:S(2)}) collective-permute-start(bf16[128,1024]{1,0:T(8,128)(2,1)} %reshape.203), channel_id=1, source_target_pairs={{0,1},{1,0},{2,3},{3,2},{4,5},{5,4},{6,7},{7,6},{8,9},{9,8},{10,11... | collective-permute-start | bytes 786440 | tf_op jit(solution)/shard_map/ppermute | solution.py:22
  268.5 10.7 %collective-permute-start.20 = (bf16[128,1024]{1,0:T(8,128)(2,1)}, bf16[128,1024]{1,0:T(8,128)(2,1)}, u32[]{:S(2)}, u32[]{:S(2)}) collective-permute-start(bf16[128,1024]{1,0:T(8,128)(2,1)} %collective-permute-done.19), channel_id=1, source_target_pairs={{0,1},{1,0},{2,3},{3,2},{4,5},{5,4},{6,7},{7,6},{8,9},{9,8},{10,11... | collective-permute-start | bytes 786440 | tf_op jit(solution)/shard_map/ppermute | solution.py:22
  269.7 8.7 %collective-permute-start.23 = (bf16[32,3840]{1,0:T(8,128)(2,1)S(1)}, bf16[32,3840]{1,0:T(8,128)(2,1)S(1)}, u32[]{:S(2)}, u32[]{:S(2)}) collective-permute-start(bf16[32,3840]{1,0:T(8,128)(2,1)S(1)} %fusion.127), channel_id=1, source_target_pairs={{0,16},{16,0},{1,17},{17,1},{2,18},{18,2},{3,19},{19,3},{4,20},{20... | collective-permute-start | bytes 737288 | tf_op jit(solution)/shard_map/ppermute | solution.py:22
  280.6 11.2 %copy-start.17 = (bf16[128,1024]{1,0:T(8,128)(2,1)S(1)}, bf16[128,1024]{1,0:T(8,128)(2,1)}, u32[]{:S(2)}) copy-start(bf16[128,1024]{1,0:T(8,128)(2,1)} %copy-done.16) | copy-start | bytes 786436
  280.6 11.2 %copy-start.19 = (bf16[128,1024]{1,0:T(8,128)(2,1)S(1)}, bf16[128,1024]{1,0:T(8,128)(2,1)}, u32[]{:S(2)}) copy-start(bf16[128,1024]{1,0:T(8,128)(2,1)} %copy-done.18) | copy-start | bytes 786436
  280.6 11.2 %copy-start.21 = (bf16[128,1024]{1,0:T(8,128)(2,1)S(1)}, bf16[128,1024]{1,0:T(8,128)(2,1)}, u32[]{:S(2)}) copy-start(bf16[128,1024]{1,0:T(8,128)(2,1)} %copy-done.20) | copy-start | bytes 786436
  280.6 11.2 %copy-start.25 = (bf16[128,1024]{1,0:T(8,128)(2,1)S(1)}, bf16[128,1024]{1,0:T(8,128)(2,1)}, u32[]{:S(2)}) copy-start(bf16[128,1024]{1,0:T(8,128)(2,1)} %copy-done.24) | copy-start | bytes 786436
  291.8 17.2 %copy-start.26 = (f32[1280]{0:T(1024)S(1)}, f32[1280]{0:T(1024)}, u32[]{:S(2)}) copy-start(f32[1280]{0:T(1024)} %param.16) | copy-start | bytes 15364
  309.0 11.0 %copy-start.1 = (bf16[1,128,3840]{2,1,0:T(8,128)(2,1)S(1)}, bf16[1,128,3840]{2,1,0:T(8,128)(2,1)}, u32[]{:S(2)}) copy-start(bf16[1,128,3840]{2,1,0:T(8,128)(2,1)} %param.15) | copy-start | bytes 2949124
Sparse Core Ops, SparseCore 0:
  38.5 32.9 all-gather.5
  279.3 28.6 all-gather.7
where the time goes:
time: 328 us; the launch traced here: 327 us
  waiting for transfers between devices  86 us (26%)
  matrix products  62.7 us (19%)
  blocking collectives  40.2 us (12%)
  local copies, waits for them, and re-layouts  40 us (12%)
  Pallas kernels  35.9 us (11%)
  between operations  26.6 us (8%)
  other arithmetic  21.2 us (6%)
  starting transfers between devices  14.1 us (4%)
    ppermute x24, waiting for transfers between devices, swap(): return lax.ppermute(value, axis, [(i, i ^ bit) for i in range(count)])  70.8 us
    pallas_call x4, Pallas kernels, streamed(): pl.pallas_call(functools.partial(streamed_kernel, dims, depth), grid=(wid...  35.9 us
    dot_general x7, matrix products, times_transposed(): lax.dot_general(value, weight, (((1,), (1,)), ((), ())), preferred_elemen...  28.5 us
    all_gather x1, blocking collectives, local(): column = lax.all_gather(sent, 'dp', axis=0, tiled=False)  23.9 us
    unnamed x76, local copies, waits for them, and re-layouts  21.9 us
    dot_general x5, matrix products, dot(): return jnp.dot(value, weight, preferred_element_type=F32)  16.8 us
    all_gather x1, waiting for transfers between devices, local(): lax.all_gather(jnp.pad(returned.astype(BF), ((0, 0), (0, back_pad))), 'dp...  15.2 us
    ppermute x24, starting transfers between devices, swap(): return lax.ppermute(value, axis, [(i, i ^ bit) for i in range(count)])  14.1 us
  transfers between devices with their start and end apart: 26, of which 15 were waited for; matrix products, arithmetic and copies ran while one was open for 18% of the time, Pallas kernels for 6%

commit v1 on v0

--- a/solution.py
+++ b/solution.py
@@ -122,7 +122,7 @@
         in_specs=[pl.BlockSpec(value.shape, lambda i: (0, 0)), w_spec],
         out_specs=pl.BlockSpec((rows, block), lambda i: (0, i)),
         out_shape=jax.ShapeDtypeStruct((rows, width), dtype),
-        compiler_params=pltpu.CompilerParams(vmem_limit_bytes=24 * 2**20),
+        compiler_params=pltpu.CompilerParams(vmem_limit_bytes=52 * 2**20),
         cost_estimate=pl.CostEstimate(
             flops=2 * rows * width * depth,
             bytes_accessed=2 * (width * depth + rows * depth) + 4 * rows * width,
@@ -223,8 +223,8 @@
     out_cot = (scale * grad_rows.astype(F32)).astype(BF)
     early = lax.cond(
         first,
-        lambda: streamed(text_rows, query_weight, False, F32),
-        lambda: streamed(out_cot, out_weight, True, F32),
+        lambda: dot(text_rows, query_weight),
+        lambda: times_transposed(out_cot, out_weight),
     )
     early_sum = scatter_columns(early).astype(BF)
 
@@ -267,15 +267,6 @@
     kv_cot = jnp.where(first, kv_cot_early, kv_cot_late)
     kv_cot = jnp.stack([pick(kv_cot, slot_of[i]) for i in range(segments)])
     kv_all = lax.all_gather(kv_cot.reshape(segments * rows_img, 2 * per), "mp", axis=0)
-    near, far = gather_pairs(flat(query_cot))
-    high = member_id // 2
-    gathered = jnp.concatenate(
-        [jnp.where(high == 0, near, far), jnp.where(high == 0, far, near)], axis=1
-    )
-    query_back = streamed(gathered, query_weight, True, F32)
-    cot_early = (jnp.concatenate(cot_in, axis=1).astype(F32) + query_back).astype(BF)
-    grads = jnp.where(first, cot_early, jnp.concatenate(cot_late, axis=1))
-
     key_all = kv_all[:, :, :per].transpose(1, 0, 2).reshape(-1, kv_width)
     value_all = kv_all[:, :, per:].transpose(1, 0, 2).reshape(-1, kv_width)
     feature_cot = (
@@ -283,10 +274,19 @@
     ).astype(BF)
     norm_part = streamed(feature_cot, projector, True, F32)
     parts = norm_part.reshape(segments, members, share, proj_in).transpose(1, 0, 2, 3)
-    summed = scatter_sum(parts)
+    summed, query_cot = lax.optimization_barrier((scatter_sum(parts), query_cot))
     returned = pick(summed, segment_id) + swap(
         pick(summed, 1 - segment_id).astype(BF), "segment", 1
     ).astype(F32)
+    near, far = gather_pairs(flat(query_cot))
+    high = member_id // 2
+    gathered = jnp.concatenate(
+        [jnp.where(high == 0, near, far), jnp.where(high == 0, far, near)], axis=1
+    )
+    query_back = streamed(gathered, query_weight, True, F32)
+    cot_early = (jnp.concatenate(cot_in, axis=1).astype(F32) + query_back).astype(BF)
+    grads = jnp.where(first, cot_early, jnp.concatenate(cot_late, axis=1))
+
     back_pad = (-proj_in) % BACK_LANES
     column = lax.all_gather(
         jnp.pad(returned.astype(BF), ((0, 0), (0, back_pad))), "dp", axis=0, tiled=False

time: 328 us -> 323 us (0.985)
  local copies, waits for them, and re-layouts: 40 us -> 29.8 us
  matrix products: 62.7 us -> 71.5 us
  waiting for transfers between devices: 86 us -> 82.2 us
    unnamed x76, local copies, waits for them, and re-layouts: 21.9 us -> 10.8 us
    dot_general x5 -> x6, matrix products: 16.8 us -> 25 us  [dot(): return jnp.dot(value, weight, preferred_element_type=F32)]
    pallas_call x4 -> x3, Pallas kernels: 35.9 us -> 36.1 us  [streamed(): pl.pallas_call(functools.partial(streamed_kernel, dims, depth), grid=(wid...]
  transfers between devices with their start and end apart: 26 -> 26, of which waited for: 15 -> 17; matrix products, arithmetic and copies ran while one was open for 18% -> 20% of each run, Pallas kernels for 6% -> 4%
where the time goes in v1:
time: 323 us; the launch traced here: 321 us
  waiting for transfers between devices  82.2 us (25%)
  matrix products  71.5 us (22%)
  blocking collectives  40.1 us (12%)
  Pallas kernels  36.1 us (11%)
  local copies, waits for them, and re-layouts  29.8 us (9%)
  between operations  26.6 us (8%)
  other arithmetic  22.5 us (7%)
  starting transfers between devices  12.6 us (4%)
    ppermute x24, waiting for transfers between devices, swap(): return lax.ppermute(value, axis, [(i, i ^ bit) for i in range(count)])  67.6 us
    pallas_call x3, Pallas kernels, streamed(): pl.pallas_call(functools.partial(streamed_kernel, dims, depth), grid=(wid...  36.1 us
    dot_general x7, matrix products, times_transposed(): lax.dot_general(value, weight, (((1,), (1,)), ((), ())), preferred_elemen...  28.5 us
    dot_general x6, matrix products, dot(): return jnp.dot(value, weight, preferred_element_type=F32)  25 us
    all_gather x1, blocking collectives, local(): column = lax.all_gather(sent, 'dp', axis=0, tiled=False)  23.9 us
    all_gather x1, waiting for transfers between devices, local(): lax.all_gather(jnp.pad(returned.astype(BF), ((0, 0), (0, back_pad))), 'dp...  14.5 us
    ppermute x24, starting transfers between devices, swap(): return lax.ppermute(value, axis, [(i, i ^ bit) for i in range(count)])  12.5 us
    unnamed x76, local copies, waits for them, and re-layouts  10.8 us
  transfers between devices with their start and end apart: 26, of which 17 were waited for; matrix products, arithmetic and copies ran while one was open for 20% of the time, Pallas kernels for 4%

profile of v1, /device:TPU:0, one launch (start us, length us, event | category | flops | bytes accessed | tf_op | source)
XLA Modules:
  0.0 321.3 jit_solution(2383178101801204419)
XLA Ops:
  7.3 1.1 copy-done
  11.0 23.9 %all-gather = bf16[128,3968]{1,0:T(8,128)(2,1)S(1)} all-gather(bf16[32,3968]{1,0:T(8,128)(2,1)S(1)} %maximum_maximum_fusion), channel_id=2, replica_groups=mesh['segment'=2,'dp'=4,'mp'=4] {'dp'}, dimensions={0}, use_global_device_ids=true | all-gather | bytes 1269760 | tf_op jit(solution)/shard_map/all_gather | solution.py:203
  40.3 8.2 %conditional.1 = (f32[128,4096]{1,0:T(8,128)S(1)}) conditional(s32[]{:T(128)} %convert_element_type.206, (bf16[128,2048]{1,0:T(8,128)(2,1)}, bf16[4096,2048]{1,0:T(8,128)(2,1)}) %tuple.51, (bf16[128,2048]{1,0:T(8,128)(2,1)S(1)}, bf16[2048,4096]{1,0:T(8,128)(2,1)}) %tuple.52), branch_computations={%region_4.5_spmd, %region_5.6_spmd} | conditional | flops 2147483648 | bytes 19398664 | solution.py:224
  40.3 8.2 %fusion.188 = f32[128,4096]{1,0:T(8,128)S(1)} fusion(bf16[128,2048]{1,0:T(8,128)(2,1)S(1)} %get-tuple-element.13, bf16[2048,4096]{1,0:T(8,128)(2,1)} %get-tuple-element.14), kind=kOutput, calls=%fused_computation.255 | convolution fusion | flops 2147483648 | bytes 19398656 | tf_op jit(solution)/shard_map/cond/branch_1_fun/dot_general | solution.py:102
  48.5 1.3 copy-done.4
  50.8 2.2 collective-permute-done
  53.0 1.1 convert_element_type.209
  55.2 1.8 add_convert_fusion.6
  57.0 1.5 collective-permute-start.1
  58.5 2.5 copy.91
  61.0 4.0 %copy.92 = bf16[512,2048]{1,0:T(8,128)(2,1)} copy(bf16[512,2048]{0,1:T(8,128)(2,1)} %bitcast.196) | data formatting | bytes 4194304 | tf_op jit(solution)/shard_map/dot_general | solution.py:239
  65.0 5.2 %collective-permute-done.1 = bf16[128,1024]{1,0:T(8,128)(2,1)S(1)} collective-permute-done((bf16[128,1024]{1,0:T(8,128)(2,1)}, bf16[128,1024]{1,0:T(8,128)(2,1)S(1)}, u32[]{:S(2)}, u32[]{:S(2)}) %collective-permute-start.1) | collective-permute-done | bytes 262176 | tf_op jit(solution)/shard_map/ppermute | solution.py:22
  70.2 2.0 add_convert_fusion.5
  74.8 11.1 %shard_map.140 = bf16[256,2048]{1,0:T(8,128)(2,1)S(1)} custom-call(bf16[256,3968]{1,0:T(8,128)(2,1)} %bitcast.208, bf16[3840,2048]{1,0:T(8,128)(2,1)} %w_ref.3), custom_call_target="tpu_custom_call" | custom-call | flops 4026531840 | bytes 19791872 | tf_op jit(solution)/shard_map/pallas_call | solution.py:119
  94.6 1.2 bitcast_add_fusion.2
  96.3 5.5 %collective-permute-done.3 = bf16[2,256,128]{2,1,0:T(8,128)(2,1)S(1)} collective-permute-done((bf16[2,256,128]{2,1,0:T(8,128)(2,1)S(1)}, bf16[2,256,128]{2,1,0:T(8,128)(2,1)S(1)}, u32[]{:S(2)}, u32[]{:S(2)}) %collective-permute-start.3) | collective-permute-done | bytes 131104 | tf_op jit(solution)/shard_map/ppermute | solution.py:22
  101.9 1.1 fusion.185
  103.0 1.2 convolution_convert_fusion.2
  105.7 7.7 %collective-permute-done.5 = bf16[128,1024]{1,0:T(8,128)(2,1)} collective-permute-done((bf16[128,1024]{1,0:T(8,128)(2,1)S(1)}, bf16[128,1024]{1,0:T(8,128)(2,1)}, u32[]{:S(2)}, u32[]{:S(2)}) %collective-permute-start.5) | collective-permute-done | bytes 262176 | tf_op jit(solution)/shard_map/ppermute | solution.py:22
  113.5 1.1 broadcast_select_fusion.13
  114.6 4.8 %fusion.14 = f32[128,2048]{1,0:T(8,128)S(1)} fusion(bf16[1,4096,2048]{2,1,0:T(8,128)(2,1)} %param.25, s32[]{:T(128)S(6)} %select_n.264, bf16[128,1024]{1,0:T(8,128)(2,1)S(1)} %get-tuple-element.48, bf16[128,1024]{1,0:T(8,128)(2,1)S(1)} %get-tuple-element.47), kind=kOutput, calls=%fused_computation.14 | convolution fusion | flops 1074790400 | bytes 9961476 | tf_op jit(solution)/shard_map/dot_general | solution.py:102
  120.4 3.0 fusion.86
  123.4 1.5 collective-permute-start.8
  125.0 3.0 fusion.89
  128.9 3.7 %collective-permute-done.8 = bf16[128,1024]{1,0:T(8,128)(2,1)S(1)} collective-permute-done((bf16[128,1024]{1,0:T(8,128)(2,1)S(1)}, bf16[128,1024]{1,0:T(8,128)(2,1)S(1)}, u32[]{:S(2)}, u32[]{:S(2)}) %collective-permute-start.8) | collective-permute-done | bytes 262176 | tf_op jit(solution)/shard_map/ppermute | solution.py:22
  132.6 4.7 %fusion.10 = f32[128,4096]{1,0:T(8,128)S(1)} fusion(bf16[128,1024]{1,0:T(8,128)(2,1)S(1)} %collective-permute-done.8, bf16[1,2048,4096]{2,1,0:T(8,128)(2,1)} %param.22), kind=kOutput, calls=%fused_computation.10 | convolution fusion | flops 1073741824 | bytes 10747904 | tf_op jit(solution)/shard_map/dot_general | solution.py:102
  137.9 1.3 fusion.20
  139.4 1.9 collective-permute-done.9
  142.9 7.0 %collective-permute-done.10 = bf16[128,1024]{1,0:T(8,128)(2,1)S(1)} collective-permute-done((bf16[128,1024]{1,0:T(8,128)(2,1)S(1)}, bf16[128,1024]{1,0:T(8,128)(2,1)S(1)}, u32[]{:S(2)}, u32[]{:S(2)}) %collective-permute-start.10) | collective-permute-done | bytes 262176 | tf_op jit(solution)/shard_map/ppermute | solution.py:22
  150.2 1.1 fusion.186
  151.3 2.8 convolution_convert_fusion.1
  155.5 7.2 %collective-permute-done.12 = bf16[128,1024]{1,0:T(8,128)(2,1)S(1)} collective-permute-done((bf16[128,1024]{1,0:T(8,128)(2,1)S(1)}, bf16[128,1024]{1,0:T(8,128)(2,1)S(1)}, u32[]{:S(2)}, u32[]{:S(2)}) %collective-permute-start.12) | collective-permute-done | bytes 262176 | tf_op jit(solution)/shard_map/ppermute | solution.py:22
  162.8 6.4 %fusion.8 = f32[128,2048]{1,0:T(8,128)S(1)} fusion(bf16[1,2048,4096]{2,1,0:T(8,128)(2,1)} %param.22, s32[]{:T(128)S(6)} %select_n.264, bf16[128,1024]{1,0:T(8,128)(2,1)S(1)} %get-tuple-element.44, bf16[128,1024]{1,0:T(8,128)(2,1)S(1)} %get-tuple-element.43), kind=kOutput, calls=%fused_computation.8 | convolution fusion | flops 1074790400 | bytes 9961476 | tf_op jit(solution)/shard_map/dot_general | solution.py:154
  169.3 4.0 %fusion.92 = bf16[128,1024]{1,0:T(8,128)(2,1)S(1)} fusion(bf16[1,2048,4096]{2,1,0:T(8,128)(2,1)} %param.22, s32[]{:T(128)S(6)} %select_n.267, f32[128,2048]{1,0:T(8,128)S(1)} %fusion.8, bf16[128,1024]{1,0:T(8,128)(2,1)S(1)} %get-tuple-element.42, bf16[128,1024]{1,0:T(8,128)(2,1)S(1)} %get-tuple-element.41, bf16[128,2048]{1,0:T(8,128)(2,1)S(1)} %bitcast.203), kind=kOutput, calls=%fused_computation.71 | convolution fusion | flops 538443776 | bytes 5767172 | tf_op jit(solution)/shard_map/dot_general | solution.py:154
  173.3 1.5 collective-permute-start.15
  174.8 3.7 %fusion.95 = bf16[128,1024]{1,0:T(8,128)(2,1)S(1)} fusion(bf16[1,2048,4096]{2,1,0:T(8,128)(2,1)} %param.22, s32[]{:T(128)S(6)} %select_n.267, f32[128,2048]{1,0:T(8,128)S(1)} %fusion.8, bf16[128,1024]{1,0:T(8,128)(2,1)S(1)} %get-tuple-element.42, bf16[128,1024]{1,0:T(8,128)(2,1)S(1)} %get-tuple-element.41, bf16[128,2048]{1,0:T(8,128)(2,1)S(1)} %bitcast.204), kind=kOutput, calls=%fused_computation.72 | convolution fusion | flops 538443776 | bytes 5767172 | tf_op jit(solution)/shard_map/dot_general | solution.py:154
  179.6 2.8 collective-permute-done.15
  182.5 6.4 %fusion.4 = f32[128,4096]{1,0:T(8,128)S(1)} fusion(bf16[4096,2048]{1,0:T(8,128)(2,1)} %bitcast.189, bf16[128,1024]{1,0:T(8,128)(2,1)S(1)} %collective-permute-done.15, f32[128]{0:T(128)S(1)} %mul.179), kind=kOutput, calls=%fused_computation.4 | convolution fusion | flops 1074135040 | bytes 10748416 | tf_op jit(solution)/shard_map/dot_general | solution.py:154
  189.6 2.9 fusion.23
  192.5 1.3 copy-done.3
  200.1 1.2 add_convert_fusion.2
  201.5 2.1 convolution_convert_fusion.4
  204.1 6.0 %collective-permute-done.17 = bf16[128,1024]{1,0:T(8,128)(2,1)} collective-permute-done((bf16[128,1024]{1,0:T(8,128)(2,1)S(1)}, bf16[128,1024]{1,0:T(8,128)(2,1)}, u32[]{:S(2)}, u32[]{:S(2)}) %collective-permute-start.17) | collective-permute-done | bytes 262176 | tf_op jit(solution)/shard_map/ppermute | solution.py:22
  210.2 1.4 add_convert_fusion.1
  213.2 2.2 convolution_convert_fusion.6
  215.7 6.7 %all_gather.24 = bf16[4,256,256]{2,1,0:T(8,128)(2,1)S(1)} all-gather(bf16[1,256,256]{2,1,0:T(8,128)(2,1)S(1)} %bitcast.214), channel_id=1, replica_groups=mesh['segment'=2,'dp'=4,'mp'=4] {'mp'}, dimensions={0}, use_global_device_ids=true | all-gather | bytes 655360 | tf_op jit(solution)/shard_map/all_gather | solution.py:269
  223.1 1.1 copy.94
  224.2 2.1 fusion.40
  226.5 3.0 fusion.38.x_ref
  229.4 13.6 %shard_map.141 = f32[256,3840]{1,0:T(8,128)} custom-call(bf16[256,2048]{1,0:T(8,128)(2,1)S(1)} %fusion.38.x_ref, bf16[3840,2048]{1,0:T(8,128)(2,1)} %w_ref.3), custom_call_target="tpu_custom_call" | custom-call | flops 4026531840 | bytes 20709376 | tf_op jit(solution)/shard_map/pallas_call | solution.py:119
  243.0 1.6 fusion.108
  245.1 2.2 collective-permute-done.18
  247.3 1.7 bitcast_add_fusion
  249.1 1.1 collective-permute-start.19
  250.2 3.0 convolution_convert_fusion
  253.1 9.6 %collective-permute-done.19 = bf16[2,32,3840]{2,1,0:T(8,128)(2,1)} collective-permute-done((bf16[2,32,3840]{2,1,0:T(8,128)(2,1)S(1)}, bf16[2,32,3840]{2,1,0:T(8,128)(2,1)}, u32[]{:S(2)}, u32[]{:S(2)}) %collective-permute-start.19) | collective-permute-done | bytes 491552 | tf_op jit(solution)/shard_map/ppermute | solution.py:22
  262.7 1.1 bitcast_add_fusion.1
  263.8 1.1 reshape.207
  264.9 1.1 collective-permute-start.21
  266.0 1.5 collective-permute-start.23
  267.6 5.1 %collective-permute-done.21 = bf16[128,1024]{1,0:T(8,128)(2,1)S(1)} collective-permute-done((bf16[128,1024]{1,0:T(8,128)(2,1)S(1)}, bf16[128,1024]{1,0:T(8,128)(2,1)S(1)}, u32[]{:S(2)}, u32[]{:S(2)}) %collective-permute-start.21) | collective-permute-done | bytes 262176 | tf_op jit(solution)/shard_map/ppermute | solution.py:22
  275.6 11.5 %shard_map.142 = f32[128,2048]{1,0:T(8,128)S(1)} custom-call(bf16[128,4096]{1,0:T(8,128)(2,1)} %pad_maximum_fusion.1.x_ref, bf16[2048,4096]{1,0:T(8,128)(2,1)} %bitcast.185), custom_call_target="tpu_custom_call" | custom-call | flops 2147483648 | bytes 18874368 | tf_op jit(solution)/shard_map/pallas_call | solution.py:119
  288.1 14.5 %all-gather.8.cloned.1.call-done = bf16[128,4096]{1,0:T(8,128)(2,1)} async-done(((bf16[32,4096]{1,0:T(8,128)(2,1)}), bf16[128,4096]{1,0:T(8,128)(2,1)}) %all-gather.8.cloned.1.call-update) | async-done | bytes 1048592 | tf_op jit(solution)/shard_map/all_gather | solution.py:291
  304.0 9.6 %all_gather.27 = bf16[128,3840]{1,0:T(8,128)(2,1)S(1)} all-gather(bf16[32,3840]{1,0:T(8,128)(2,1)S(1)} %pad_maximum_fusion.13), channel_id=1, replica_groups=mesh['segment'=2,'dp'=4,'mp'=4] {'mp'}, dimensions={0}, use_global_device_ids=true | all-gather | bytes 1228800 | tf_op jit(solution)/shard_map/all_gather | solution.py:302
  (184 shorter events, 35.8 us)
Async XLA Ops:
  7.2 1.2 copy-start
  7.2 32.0 %copy-start.27 = (s32[2]{0:T(128)S(1)}, s32[2]{0:T(128)}, u32[]{:S(2)}) copy-start(s32[2]{0:T(128)} %param.21) | copy-start | bytes 28
  7.2 32.1 %copy-start.9 = (bf16[2,64,2048]{2,1,0:T(8,128)(2,1)S(1)}, bf16[2,64,2048]{2,1,0:T(8,128)(2,1)}, u32[]{:S(2)}) copy-start(bf16[2,64,2048]{2,1,0:T(8,128)(2,1)} %param.27) | copy-start | bytes 1572868
  7.2 66.1 %all-gather.6.cloned.1.call-start = ((), (), s32[]{:S(2)}) async-start(), calls=%async_computation | async-start | bytes 2285568 | tf_op jit(solution)/shard_map/all_gather | solution.py:206
  8.5 31.7 %copy-start.8 = (bf16[2,64,2048]{2,1,0:T(8,128)(2,1)S(1)}, bf16[2,64,2048]{2,1,0:T(8,128)(2,1)}, u32[]{:S(2)}) copy-start(bf16[2,64,2048]{2,1,0:T(8,128)(2,1)} %param.20) | copy-start | bytes 1572868
  38.4 264.2 %all-gather.8.cloned.1.call-start = ((), (), s32[]{:S(2)}) async-start(), calls=%async_computation.1 | async-start | bytes 1310720 | tf_op jit(solution)/shard_map/all_gather | solution.py:291
  48.5 1.3 copy-start.4
  49.9 8.6 %copy-start.2 = (bf16[1,2048,512]{2,1,0:T(8,128)(2,1)S(1)}, bf16[1,2048,512]{2,1,0:T(8,128)(2,1)}, u32[]{:S(2)}) copy-start(bf16[1,2048,512]{2,1,0:T(8,128)(2,1)} %param.23) | copy-start | bytes 6291460
  50.8 2.3 collective-permute-start
  54.2 1.1 copy-start.5
  57.0 13.2 %collective-permute-start.1 = (bf16[128,1024]{1,0:T(8,128)(2,1)}, bf16[128,1024]{1,0:T(8,128)(2,1)S(1)}, u32[]{:S(2)}, u32[]{:S(2)}) collective-permute-start(bf16[128,1024]{1,0:T(8,128)(2,1)} %add_convert_fusion.6), channel_id=1, source_target_pairs={{0,2},{1,3},{2,0},{3,1},{4,6},{5,7},{6,4},{7,5},{8,10},{9,11},{10,... | collective-permute-start | bytes 786440 | tf_op jit(solution)/shard_map/ppermute | solution.py:22
  73.3 29.8 %copy-start.13 = (bf16[2,512,128]{2,1,0:T(8,128)(2,1)}, bf16[2,512,128]{2,1,0:T(8,128)(2,1)S(1)}, u32[]{:S(2)}) copy-start(bf16[2,512,128]{2,1,0:T(8,128)(2,1)S(1)} %reshape.196) | copy-start | bytes 786436
  74.8 11.1 %copy-start.12 = (bf16[512,2048]{1,0:T(8,128)(2,1)S(1)}, bf16[512,2048]{1,0:T(8,128)(2,1)}, u32[]{:S(2)}) copy-start(bf16[512,2048]{1,0:T(8,128)(2,1)} %copy.91) | copy-start | bytes 6291460
  85.9 1.6 copy-start.11
  88.3 1.0 copy-start.7
  90.1 4.6 %collective-permute-start.2 = (bf16[2,2,256,128]{3,2,0,1:T(8,128)(2,1)}, bf16[2,2,256,128]{3,2,0,1:T(8,128)(2,1)}, u32[]{:S(2)}, u32[]{:S(2)}) collective-permute-start(bf16[2,2,256,128]{3,2,0,1:T(8,128)(2,1)} %fusion.118), channel_id=1, source_target_pairs={{0,1},{1,0},{2,3},{3,2},{4,5},{5,4},{6,7},{7,6},{8,9},{9,8},{10,11... | collective-permute-start | bytes 786440 | tf_op jit(solution)/shard_map/ppermute | solution.py:22
  95.9 6.0 %collective-permute-start.3 = (bf16[2,256,128]{2,1,0:T(8,128)(2,1)S(1)}, bf16[2,256,128]{2,1,0:T(8,128)(2,1)S(1)}, u32[]{:S(2)}, u32[]{:S(2)}) collective-permute-start(bf16[2,256,128]{2,1,0:T(8,128)(2,1)S(1)} %fusion.140), channel_id=1, source_target_pairs={{0,2},{1,3},{2,0},{3,1},{4,6},{5,7},{6,4},{7,5},{8,10},{9,11},{10,... | collective-permute-start | bytes 393224 | tf_op jit(solution)/shard_map/ppermute | solution.py:22
  105.3 8.1 %copy-start.15 = (bf16[128,1024]{1,0:T(8,128)(2,1)}, bf16[128,1024]{1,0:T(8,128)(2,1)S(1)}, u32[]{:S(2)}) copy-start(bf16[128,1024]{1,0:T(8,128)(2,1)S(1)} %reshape.199) | copy-start | bytes 786436
  105.4 8.1 %collective-permute-start.5 = (bf16[128,1024]{1,0:T(8,128)(2,1)S(1)}, bf16[128,1024]{1,0:T(8,128)(2,1)}, u32[]{:S(2)}, u32[]{:S(2)}) collective-permute-start(bf16[128,1024]{1,0:T(8,128)(2,1)S(1)} %reshape.199), channel_id=1, source_target_pairs={{0,2},{1,3},{2,0},{3,1},{4,6},{5,7},{6,4},{7,5},{8,10},{9,11},{10,... | collective-permute-start | bytes 786440 | tf_op jit(solution)/shard_map/ppermute | solution.py:22
  105.7 7.7 %collective-permute-start.4 = (bf16[128,1024]{1,0:T(8,128)(2,1)S(1)}, bf16[128,1024]{1,0:T(8,128)(2,1)}, u32[]{:S(2)}, u32[]{:S(2)}) collective-permute-start(bf16[128,1024]{1,0:T(8,128)(2,1)S(1)} %reshape.199), channel_id=1, source_target_pairs={{0,1},{1,0},{2,3},{3,2},{4,5},{5,4},{6,7},{7,6},{8,9},{9,8},{10,11... | collective-permute-start | bytes 786440 | tf_op jit(solution)/shard_map/ppermute | solution.py:22
  113.5 5.9 %collective-permute-start.6 = (bf16[128,1024]{1,0:T(8,128)(2,1)}, bf16[128,1024]{1,0:T(8,128)(2,1)S(1)}, u32[]{:S(2)}, u32[]{:S(2)}) collective-permute-start(bf16[128,1024]{1,0:T(8,128)(2,1)} %collective-permute-done.5), channel_id=1, source_target_pairs={{0,1},{1,0},{2,3},{3,2},{4,5},{5,4},{6,7},{7,6},{8,9},{9,8},{10,11... | collective-permute-start | bytes 786440 | tf_op jit(solution)/shard_map/ppermute | solution.py:22
  114.5 23.3 %slice-start = ((s8[16777216]{0:T(1024)(128)(4,1)}), s8[4194304]{0:T(1024)(128)(4,1)S(1)}, s32[]{:S(2)}) async-start(s8[16777216]{0:T(1024)(128)(4,1)} %bitcast.186), calls=%async_computation.2 | async-start | bytes 8388608
  114.6 23.3 %slice-start.1 = ((s8[16777216]{0:T(1024)(128)(4,1)}), s8[4194304]{0:T(1024)(128)(4,1)S(1)}, s32[]{:S(2)}) async-start(s8[16777216]{0:T(1024)(128)(4,1)} %bitcast.186), calls=%async_computation.3 | async-start | bytes 8388608
  123.4 14.4 %slice-start.2 = ((s8[16777216]{0:T(1024)(128)(4,1)}), s8[4194304]{0:T(1024)(128)(4,1)S(1)}, s32[]{:S(2)}) async-start(s8[16777216]{0:T(1024)(128)(4,1)} %bitcast.186), calls=%async_computation.4 | async-start | bytes 8388608
  123.4 9.2 %collective-permute-start.8 = (bf16[128,1024]{1,0:T(8,128)(2,1)S(1)}, bf16[128,1024]{1,0:T(8,128)(2,1)S(1)}, u32[]{:S(2)}, u32[]{:S(2)}) collective-permute-start(bf16[128,1024]{1,0:T(8,128)(2,1)S(1)} %fusion.86), channel_id=1, source_target_pairs={{0,16},{16,0},{1,17},{17,1},{2,18},{18,2},{3,19},{19,3},{4,20},{20... | collective-permute-start | bytes 786440 | tf_op jit(solution)/shard_map/ppermute | solution.py:22
  128.0 9.9 %slice-start.3 = ((s8[16777216]{0:T(1024)(128)(4,1)}), s8[4194304]{0:T(1024)(128)(4,1)S(1)}, s32[]{:S(2)}) async-start(s8[16777216]{0:T(1024)(128)(4,1)} %bitcast.186), calls=%async_computation.5 | async-start | bytes 8388608
  128.0 9.8 %collective-permute-start.7 = (bf16[128,1024]{1,0:T(8,128)(2,1)S(1)}, bf16[128,1024]{1,0:T(8,128)(2,1)S(1)}, u32[]{:S(2)}, u32[]{:S(2)}) collective-permute-start(bf16[128,1024]{1,0:T(8,128)(2,1)S(1)} %fusion.89), channel_id=1, source_target_pairs={{0,16},{16,0},{1,17},{17,1},{2,18},{18,2},{3,19},{19,3},{4,20},{20... | collective-permute-start | bytes 786440 | tf_op jit(solution)/shard_map/ppermute | solution.py:22
  139.3 2.6 copy-start.14
  139.3 2.0 collective-permute-start.9
  141.5 8.4 %collective-permute-start.10 = (bf16[128,1024]{1,0:T(8,128)(2,1)S(1)}, bf16[128,1024]{1,0:T(8,128)(2,1)S(1)}, u32[]{:S(2)}, u32[]{:S(2)}) collective-permute-start(bf16[128,1024]{1,0:T(8,128)(2,1)S(1)} %add_convert_fusion.4), channel_id=1, source_target_pairs={{0,2},{1,3},{2,0},{3,1},{4,6},{5,7},{6,4},{7,5},{8,10},{9,11},{10,... | collective-permute-start | bytes 786440 | tf_op jit(solution)/shard_map/ppermute | solution.py:22
  150.1 4.9 %copy-start.22 = (bf16[2,512,128]{2,1,0:T(8,128)(2,1)}, bf16[2,512,128]{2,1,0:T(8,128)(2,1)S(1)}, u32[]{:S(2)}) copy-start(bf16[2,512,128]{2,1,0:T(8,128)(2,1)S(1)} %reshape.200) | copy-start | bytes 786436
  155.1 7.6 %collective-permute-start.12 = (bf16[128,1024]{1,0:T(8,128)(2,1)S(1)}, bf16[128,1024]{1,0:T(8,128)(2,1)S(1)}, u32[]{:S(2)}, u32[]{:S(2)}) collective-permute-start(bf16[128,1024]{1,0:T(8,128)(2,1)S(1)} %reshape.201), channel_id=1, source_target_pairs={{0,2},{1,3},{2,0},{3,1},{4,6},{5,7},{6,4},{7,5},{8,10},{9,11},{10,... | collective-permute-start | bytes 786440 | tf_op jit(solution)/shard_map/ppermute | solution.py:22
  155.5 7.2 %collective-permute-start.11 = (bf16[128,1024]{1,0:T(8,128)(2,1)S(1)}, bf16[128,1024]{1,0:T(8,128)(2,1)S(1)}, u32[]{:S(2)}, u32[]{:S(2)}) collective-permute-start(bf16[128,1024]{1,0:T(8,128)(2,1)S(1)} %reshape.201), channel_id=1, source_target_pairs={{0,1},{1,0},{2,3},{3,2},{4,5},{5,4},{6,7},{7,6},{8,9},{9,8},{10,11... | collective-permute-start | bytes 786440 | tf_op jit(solution)/shard_map/ppermute | solution.py:22
  162.7 6.5 %collective-permute-start.13 = (bf16[128,1024]{1,0:T(8,128)(2,1)S(1)}, bf16[128,1024]{1,0:T(8,128)(2,1)S(1)}, u32[]{:S(2)}, u32[]{:S(2)}) collective-permute-start(bf16[128,1024]{1,0:T(8,128)(2,1)S(1)} %collective-permute-done.12), channel_id=1, source_target_pairs={{0,1},{1,0},{2,3},{3,2},{4,5},{5,4},{6,7},{7,6},{8,9},{9,8},{10,11... | collective-permute-start | bytes 786440 | tf_op jit(solution)/shard_map/ppermute | solution.py:22
  162.7 6.6 %copy-start.10 = (bf16[2,64,2048]{2,1,0:T(8,128)(2,1)S(1)}, bf16[2,64,2048]{2,1,0:T(8,128)(2,1)}, u32[]{:S(2)}) copy-start(bf16[2,64,2048]{2,1,0:T(8,128)(2,1)} %param.27) | copy-start | bytes 1572868
  162.7 26.8 %slice-start.4 = ((s8[16777216]{0:T(1024)(128)(4,1)}), s8[4194304]{0:T(1024)(128)(4,1)S(1)}, s32[]{:S(2)}) async-start(s8[16777216]{0:T(1024)(128)(4,1)} %bitcast.190), calls=%async_computation.6 | async-start | bytes 8388608
  162.8 26.8 %slice-start.5 = ((s8[16777216]{0:T(1024)(128)(4,1)}), s8[4194304]{0:T(1024)(128)(4,1)S(1)}, s32[]{:S(2)}) async-start(s8[16777216]{0:T(1024)(128)(4,1)} %bitcast.190), calls=%async_computation.7 | async-start | bytes 8388608
  173.3 5.3 %copy-start.16 = (bf16[128,1024]{1,0:T(8,128)(2,1)}, bf16[128,1024]{1,0:T(8,128)(2,1)S(1)}, u32[]{:S(2)}) copy-start(bf16[128,1024]{1,0:T(8,128)(2,1)S(1)} %fusion.92) | copy-start | bytes 786436
  173.3 16.3 %slice-start.6 = ((s8[16777216]{0:T(1024)(128)(4,1)}), s8[4194304]{0:T(1024)(128)(4,1)S(1)}, s32[]{:S(2)}) async-start(s8[16777216]{0:T(1024)(128)(4,1)} %bitcast.190), calls=%async_computation.8 | async-start | bytes 8388608
  173.3 9.2 %collective-permute-start.15 = (bf16[128,1024]{1,0:T(8,128)(2,1)S(1)}, bf16[128,1024]{1,0:T(8,128)(2,1)S(1)}, u32[]{:S(2)}, u32[]{:S(2)}) collective-permute-start(bf16[128,1024]{1,0:T(8,128)(2,1)S(1)} %fusion.92), channel_id=1, source_target_pairs={{0,16},{16,0},{1,17},{17,1},{2,18},{18,2},{3,19},{19,3},{4,20},{20... | collective-permute-start | bytes 786440 | tf_op jit(solution)/shard_map/ppermute | solution.py:22
  178.6 10.3 %copy-start.18 = (bf16[128,1024]{1,0:T(8,128)(2,1)}, bf16[128,1024]{1,0:T(8,128)(2,1)S(1)}, u32[]{:S(2)}) copy-start(bf16[128,1024]{1,0:T(8,128)(2,1)S(1)} %fusion.95) | copy-start | bytes 786436
  178.6 11.0 %slice-start.7 = ((s8[16777216]{0:T(1024)(128)(4,1)}), s8[4194304]{0:T(1024)(128)(4,1)S(1)}, s32[]{:S(2)}) async-start(s8[16777216]{0:T(1024)(128)(4,1)} %bitcast.190), calls=%async_computation.9 | async-start | bytes 8388608
  178.6 10.3 %collective-permute-start.14 = (bf16[128,1024]{1,0:T(8,128)(2,1)S(1)}, bf16[128,1024]{1,0:T(8,128)(2,1)S(1)}, u32[]{:S(2)}, u32[]{:S(2)}) collective-permute-start(bf16[128,1024]{1,0:T(8,128)(2,1)S(1)} %fusion.95), channel_id=1, source_target_pairs={{0,16},{16,0},{1,17},{17,1},{2,18},{18,2},{3,19},{19,3},{4,20},{20... | collective-permute-start | bytes 786440 | tf_op jit(solution)/shard_map/ppermute | solution.py:22
  182.5 6.4 %copy-start.24 = (bf16[128,1024]{1,0:T(8,128)(2,1)}, bf16[128,1024]{1,0:T(8,128)(2,1)S(1)}, u32[]{:S(2)}) copy-start(bf16[128,1024]{1,0:T(8,128)(2,1)S(1)} %collective-permute-done.15) | copy-start | bytes 786436
  188.9 0.7 copy-start.20
  192.5 1.3 copy-start.3
  194.7 4.3 %collective-permute-start.16 = (bf16[128,2048]{1,0:T(8,128)(2,1)}, bf16[128,2048]{1,0:T(8,128)(2,1)S(1)}, u32[]{:S(2)}, u32[]{:S(2)}) collective-permute-start(bf16[128,2048]{1,0:T(8,128)(2,1)} %pad_maximum_fusion.6), channel_id=1, source_target_pairs={{0,1},{1,0},{2,3},{3,2},{4,5},{5,4},{6,7},{7,6},{8,9},{9,8},{10,11... | collective-permute-start | bytes 1572872 | tf_op jit(solution)/shard_map/ppermute | solution.py:22
  199.1 1.0 copy-start.6
  200.1 3.5 %copy-start.23 = (bf16[2,512,128]{2,1,0:T(8,128)(2,1)S(1)}, bf16[2,512,128]{2,1,0:T(8,128)(2,1)}, u32[]{:S(2)}) copy-start(bf16[2,512,128]{2,1,0:T(8,128)(2,1)} %copy-done.22) | copy-start | bytes 786436
  201.3 8.9 %collective-permute-start.17 = (bf16[128,1024]{1,0:T(8,128)(2,1)S(1)}, bf16[128,1024]{1,0:T(8,128)(2,1)}, u32[]{:S(2)}, u32[]{:S(2)}) collective-permute-start(bf16[128,1024]{1,0:T(8,128)(2,1)S(1)} %add_convert_fusion.2), channel_id=1, source_target_pairs={{0,2},{1,3},{2,0},{3,1},{4,6},{5,7},{6,4},{7,5},{8,10},{9,11},{10,... | collective-permute-start | bytes 786440 | tf_op jit(solution)/shard_map/ppermute | solution.py:22
  244.7 2.6 collective-permute-start.18
  249.1 13.6 %collective-permute-start.19 = (bf16[2,32,3840]{2,1,0:T(8,128)(2,1)S(1)}, bf16[2,32,3840]{2,1,0:T(8,128)(2,1)}, u32[]{:S(2)}, u32[]{:S(2)}) collective-permute-start(bf16[2,32,3840]{2,1,0:T(8,128)(2,1)S(1)} %fusion.116), channel_id=1, source_target_pairs={{0,2},{1,3},{2,0},{3,1},{4,6},{5,7},{6,4},{7,5},{8,10},{9,11},{10,... | collective-permute-start | bytes 1474568 | tf_op jit(solution)/shard_map/ppermute | solution.py:22
  264.9 7.8 %collective-permute-start.21 = (bf16[128,1024]{1,0:T(8,128)(2,1)S(1)}, bf16[128,1024]{1,0:T(8,128)(2,1)S(1)}, u32[]{:S(2)}, u32[]{:S(2)}) collective-permute-start(bf16[128,1024]{1,0:T(8,128)(2,1)S(1)} %reshape.207), channel_id=1, source_target_pairs={{0,2},{1,3},{2,0},{3,1},{4,6},{5,7},{6,4},{7,5},{8,10},{9,11},{10,... | collective-permute-start | bytes 786440 | tf_op jit(solution)/shard_map/ppermute | solution.py:22
  266.0 7.2 %collective-permute-start.23 = (bf16[32,3840]{1,0:T(8,128)(2,1)S(1)}, bf16[32,3840]{1,0:T(8,128)(2,1)S(1)}, u32[]{:S(2)}, u32[]{:S(2)}) collective-permute-start(bf16[32,3840]{1,0:T(8,128)(2,1)S(1)} %fusion.127), channel_id=1, source_target_pairs={{0,16},{16,0},{1,17},{17,1},{2,18},{18,2},{3,19},{19,3},{4,20},{20... | collective-permute-start | bytes 737288 | tf_op jit(solution)/shard_map/ppermute | solution.py:22
  267.6 6.4 %collective-permute-start.20 = (bf16[128,1024]{1,0:T(8,128)(2,1)S(1)}, bf16[128,1024]{1,0:T(8,128)(2,1)S(1)}, u32[]{:S(2)}, u32[]{:S(2)}) collective-permute-start(bf16[128,1024]{1,0:T(8,128)(2,1)S(1)} %reshape.207), channel_id=1, source_target_pairs={{0,1},{1,0},{2,3},{3,2},{4,5},{5,4},{6,7},{7,6},{8,9},{9,8},{10,11... | collective-permute-start | bytes 786440 | tf_op jit(solution)/shard_map/ppermute | solution.py:22
  272.7 1.5 collective-permute-start.22
  275.6 11.5 %copy-start.17 = (bf16[128,1024]{1,0:T(8,128)(2,1)S(1)}, bf16[128,1024]{1,0:T(8,128)(2,1)}, u32[]{:S(2)}) copy-start(bf16[128,1024]{1,0:T(8,128)(2,1)} %copy-done.16) | copy-start | bytes 786436
  275.6 11.5 %copy-start.19 = (bf16[128,1024]{1,0:T(8,128)(2,1)S(1)}, bf16[128,1024]{1,0:T(8,128)(2,1)}, u32[]{:S(2)}) copy-start(bf16[128,1024]{1,0:T(8,128)(2,1)} %copy-done.18) | copy-start | bytes 786436
  275.6 11.5 %copy-start.21 = (bf16[128,1024]{1,0:T(8,128)(2,1)S(1)}, bf16[128,1024]{1,0:T(8,128)(2,1)}, u32[]{:S(2)}) copy-start(bf16[128,1024]{1,0:T(8,128)(2,1)} %copy-done.20) | copy-start | bytes 786436
  275.6 11.5 %copy-start.25 = (bf16[128,1024]{1,0:T(8,128)(2,1)S(1)}, bf16[128,1024]{1,0:T(8,128)(2,1)}, u32[]{:S(2)}) copy-start(bf16[128,1024]{1,0:T(8,128)(2,1)} %copy-done.24) | copy-start | bytes 786436
  287.1 16.5 %copy-start.26 = (f32[1280]{0:T(1024)S(1)}, f32[1280]{0:T(1024)}, u32[]{:S(2)}) copy-start(f32[1280]{0:T(1024)} %param.16) | copy-start | bytes 15364
  303.6 10.9 %copy-start.1 = (bf16[1,128,3840]{2,1,0:T(8,128)(2,1)S(1)}, bf16[1,128,3840]{2,1,0:T(8,128)(2,1)}, u32[]{:S(2)}) copy-start(bf16[1,128,3840]{2,1,0:T(8,128)(2,1)} %param.15) | copy-start | bytes 2949124
Sparse Core Ops, SparseCore 0:
  38.5 32.5 all-gather.5
  274.1 28.3 all-gather.7
